TPU v7x, 256 devices: a whole 4x4x8 slice. The times are simulated.
256 devices in a mesh: seq: 32 (over z, y), head: 4 (over x), rep: 2 (over core).
Axes of the slice: x: 4, y: 4, z: 8, core: 2. Of those that a mesh axis runs over, the one named last changes fastest.
Arguments:
- byte_states: bfloat16 [2, 8192, 3072], P('rep', 'seq', 'head'), may hold values from -6 to 6
- boundary: int32 [2, 8192], P('rep', 'seq'), may hold values from 0 to 1, as said below
- confidence: float32 [2, 8192], P('rep', 'seq'), may hold values from 0.5 to 1
- query_rows: bfloat16 [2, 2048, 3072], P('rep', 'seq', 'head'), may hold values from -50 to 50
- key_rows: bfloat16 [2, 2048, 3072], P('rep', 'seq', 'head'), may hold values from -6 to 6
- value_rows: bfloat16 [2, 2048, 3072], P('rep', 'seq', 'head'), may hold values from -6 to 6
- out_weight: bfloat16 [3072, 3072], P('seq', 'head'), may hold values from -0.109375 to 0.109375
- upstream: bfloat16 [2, 8192, 3072], P('rep', 'seq', 'head'), may hold values from -6 to 6
Outputs:
- byte_grad: bfloat16 [2, 8192, 3072], P('rep', 'seq', 'head')
- confidence_grad: float32 [2, 8192], P('rep', 'seq')
- query_grad: bfloat16 [2, 2048, 3072], P('rep', 'seq', 'head')
- key_grad: bfloat16 [2, 2048, 3072], P('rep', 'seq', 'head')
- value_grad: bfloat16 [2, 2048, 3072], P('rep', 'seq', 'head')
- weight_grad: float32 [3072, 3072], P('seq', 'head')
Inputs may be any that keep to these rules, and one draw needn't show every extreme that they name: Each block of 256 bytes holds between 16 and 64 boundary bytes, in every window some block exactly 64; byte 0 of every window is a boundary byte, and the first byte of every other block is not.
All inputs are finite; a program needn't handle non-finite values.
Results may differ from a plain program's by a relative error of at most 0.04.
Values may be sent and summed in bfloat16 or wider, within the bound.
A program may use at most 128 MiB of HBM per device.

v0:
```python
import jax
import jax.numpy as jnp
from jax import lax
from jax.sharding import PartitionSpec as P

HEAD_DIM = 128


far_position = 1073741824


def carried_in(part, axis, combine, identity):
    place = lax.axis_index(axis)
    gathered = lax.all_gather(part, axis)
    state = jnp.zeros_like(part) + jnp.asarray(identity, part.dtype)

    def one(lap, state):
        return combine(state, lax.dynamic_index_in_dim(gathered, lap, 0, False))

    return lax.fori_loop(0, place, one, state)


def from_behind(shard, axis, by):
    peers = lax.axis_size(axis)
    pairs = [(i, i + by) for i in range(peers) if 0 <= i + by < peers]
    return lax.ppermute(shard, axis, pairs)


def local(
    byte_states, boundary, confidence, query_rows, key_rows, value_rows, out_weight, upstream
):
    states = byte_states[0]
    starts = boundary[0]
    conf_local = confidence[0]
    queries = query_rows[0]
    own_keys = key_rows[0]
    own_values = value_rows[0]
    cotangent = upstream[0]
    slot_count = queries.shape[0]
    feature_count = queries.shape[1]
    head_count = feature_count // HEAD_DIM
    score_scale = HEAD_DIM ** (-0.5)
    live_count = jnp.sum(starts)
    offset = carried_in(live_count, "seq", lambda earlier, later: earlier + later, jnp.int32(0))
    slot_index = jnp.arange(slot_count, dtype=jnp.int32)
    query_position = jnp.where(slot_index < live_count, offset + slot_index, far_position)
    key_position = jnp.where(slot_index < live_count, offset + slot_index, far_position + 1)
    byte_rank = jnp.cumsum(starts) - 1
    own_select = byte_rank[:, None] == slot_index[None, :]
    from_prev = byte_rank < 0
    own_round = own_select.astype(jnp.bfloat16)
    own_wide = own_select.astype(jnp.float32)
    picked = own_round * starts[:, None].astype(jnp.bfloat16)
    group_rows = jnp.einsum("bs,bd->sd", picked, states, preferred_element_type=jnp.float32)
    all_keys, all_values = (
        lax.all_gather(own_keys, "seq", axis=0, tiled=True),
        lax.all_gather(own_values, "seq", axis=0, tiled=True),
    )
    all_key_pos = lax.all_gather(key_position, "seq", axis=0, tiled=True)
    all_query_pos = jnp.where(all_key_pos > far_position, far_position, all_key_pos)
    key_total = all_keys.shape[0]
    allowed = all_key_pos[None, :] <= query_position[:, None]
    head_query = queries.reshape(slot_count, head_count, HEAD_DIM)
    head_keys = all_keys.reshape(key_total, head_count, HEAD_DIM)
    head_values = all_values.reshape(key_total, head_count, HEAD_DIM)
    scores = (
        jnp.einsum("qhd,khd->hqk", head_query, head_keys, preferred_element_type=jnp.float32)
        * score_scale
    )
    scores = jnp.where(allowed[None], scores, -jnp.inf)
    row_top = jnp.max(scores, axis=2)
    attention = jnp.exp(scores - row_top[:, :, None])
    row_total = jnp.sum(attention, axis=2)
    head_out = jnp.einsum(
        "hqk,khd->qhd",
        attention.astype(jnp.bfloat16),
        head_values,
        preferred_element_type=jnp.float32,
    )
    head_out = (head_out / row_total.T[:, :, None]).astype(jnp.bfloat16)
    attended = head_out.reshape(slot_count, feature_count)
    log_total = (row_top + jnp.log(row_total)).T
    full_weight = lax.all_gather(out_weight, "seq", axis=0, tiled=True)
    partial_value = jnp.einsum(
        "sc,oc->so", attended, full_weight, preferred_element_type=jnp.float32
    )
    projected = lax.psum_scatter(partial_value, "head", scatter_dimension=1, tiled=True)
    group_out = (group_rows + projected).astype(jnp.bfloat16)
    last_row = lax.dynamic_slice_in_dim(group_out, live_count - 1, 1, 0)
    before_row = from_behind(last_row, "seq", 1)
    byte_rows = jnp.dot(own_round, group_out, preferred_element_type=jnp.float32)
    byte_rows = byte_rows + jnp.where(from_prev[:, None], before_row.astype(jnp.float32), 0.0)
    upstream_wide = cotangent.astype(jnp.float32)
    conf_part = jnp.sum(upstream_wide * byte_rows, axis=1)
    conf_grad = lax.psum(conf_part, "head")
    weighted = conf_local[:, None] * upstream_wide
    group_grad = jnp.einsum("bs,bd->sd", own_wide, weighted, precision=lax.Precision.HIGHEST)
    spill = jnp.sum(jnp.where(from_prev[:, None], weighted, 0.0), axis=0, keepdims=True)
    spill_in = from_behind(spill, "seq", -1)
    group_grad = group_grad + jnp.where(slot_index[:, None] == live_count - 1, spill_in, 0.0)
    own_grad = jnp.dot(own_wide, group_grad, precision=lax.Precision.HIGHEST)
    byte_grad = (upstream_wide + jnp.where(starts[:, None] == 1, own_grad, 0.0)).astype(
        jnp.bfloat16
    )
    grad_round = group_grad.astype(jnp.bfloat16)
    grad_full = lax.all_gather(grad_round, "head", axis=1, tiled=True)
    out_wide = jnp.dot(grad_full, full_weight, preferred_element_type=jnp.float32)
    out_grad = out_wide.astype(jnp.bfloat16)
    grad_slots = lax.all_to_all(grad_full, "seq", split_axis=1, concat_axis=0, tiled=True)
    window_rows = jnp.einsum(
        "so,sc->oc",
        grad_slots,
        lax.all_gather(attended, "seq", axis=0, tiled=True),
        preferred_element_type=jnp.float32,
    )
    weight_grad = lax.psum(window_rows, "rep")
    head_grad = out_grad.reshape(slot_count, head_count, HEAD_DIM)
    row_dot = jnp.sum(head_grad.astype(jnp.float32) * head_out.astype(jnp.float32), axis=2)
    back_probs = jnp.exp(scores - log_total.T[:, :, None])
    flow_grad = jnp.einsum(
        "qhd,khd->hqk", head_grad, head_values, preferred_element_type=jnp.float32
    )
    dscore = (back_probs * (flow_grad - row_dot.T[:, :, None])).astype(jnp.bfloat16)
    query_grad = (
        jnp.einsum("hqk,khd->qhd", dscore, head_keys, preferred_element_type=jnp.float32)
        * score_scale
    )
    query_grad = query_grad.reshape(slot_count, feature_count).astype(jnp.bfloat16)
    stats_total, stats_dot = (
        lax.all_gather(log_total, "seq", axis=0, tiled=True),
        lax.all_gather(row_dot, "seq", axis=0, tiled=True),
    )
    mine_keys = own_keys.reshape(slot_count, head_count, HEAD_DIM)
    mine_values = own_values.reshape(slot_count, head_count, HEAD_DIM)
    piece_query = lax.all_gather(queries, "seq", axis=0, tiled=True)
    piece_grad = lax.all_gather(out_grad, "seq", axis=0, tiled=True)
    row_count = piece_query.shape[0]
    part_query = piece_query.reshape(row_count, head_count, HEAD_DIM)
    part_grad = piece_grad.reshape(row_count, head_count, HEAD_DIM)
    visible = key_position[None, :] <= all_query_pos[:, None]
    part_scores = (
        jnp.einsum("qhd,khd->hqk", part_query, mine_keys, preferred_element_type=jnp.float32)
        * score_scale
    )
    part_scores = jnp.where(visible[None], part_scores, -jnp.inf)
    part_probs = jnp.exp(part_scores - stats_total.T[:, :, None])
    acc_values = jnp.einsum(
        "hqk,qhd->khd",
        part_probs.astype(jnp.bfloat16),
        part_grad,
        preferred_element_type=jnp.float32,
    )
    part_flow = jnp.einsum(
        "qhd,khd->hqk", part_grad, mine_values, preferred_element_type=jnp.float32
    )
    part_dscore = (part_probs * (part_flow - stats_dot.T[:, :, None])).astype(jnp.bfloat16)
    acc_keys = (
        jnp.einsum("hqk,qhd->khd", part_dscore, part_query, preferred_element_type=jnp.float32)
        * score_scale
    )
    acc_keys, acc_values = (acc_keys, acc_values)
    key_grad = acc_keys.reshape(slot_count, feature_count).astype(jnp.bfloat16)
    value_grad = acc_values.reshape(slot_count, feature_count).astype(jnp.bfloat16)
    return (
        byte_grad[None],
        conf_grad[None],
        query_grad[None],
        key_grad[None],
        value_grad[None],
        weight_grad,
    )


def solution(mesh):
    return jax.shard_map(
        local,
        mesh=mesh,
        in_specs=(
            P("rep", "seq", "head"),
            P("rep", "seq"),
            P("rep", "seq"),
            P("rep", "seq", "head"),
            P("rep", "seq", "head"),
            P("rep", "seq", "head"),
            P("seq", "head"),
            P("rep", "seq", "head"),
        ),
        out_specs=(
            P("rep", "seq", "head"),
            P("rep", "seq"),
            P("rep", "seq", "head"),
            P("rep", "seq", "head"),
            P("rep", "seq", "head"),
            P("seq", "head"),
        ),
        check_vma=False,
    )
```

profile of v0, /device:TPU:68, one launch (start us, length us, event | category | flops | bytes accessed | tf_op | source)
XLA Modules:
  0.0 559.9 jit_solution(15124917575921523347)
XLA Ops:
  12.5 4.5 collective-permute-start
  22.1 19.8 %all-reduce = s32[32]{0:T(128)S(1)} all-reduce(s32[32]{0:T(128)S(1)} %dynamic-update-slice), channel_id=1, replica_groups=mesh['seq'=32,'head'=4,'rep'=2] {'seq'}, use_global_device_ids=true, to_apply=%add | all-reduce | flops 32 | bytes 256
  41.9 10.1 %while.10 = (s32[]{:T(128)}, s32[]{:T(128)}, s32[]{:T(128)}, s32[32]{0:T(128)S(1)}, s32[]{:T(128)}, /*index=5*/s32[]{:T(128)}, s32[]{:T(128)}) while((s32[]{:T(128)}, s32[]{:T(128)}, s32[]{:T(128)}, s32[32]{0:T(128)S(1)}, s32[]{:T(128)}, /*index=5*/s32[]{:T(128)}, s32[]{:T(128)}) %tuple.27), condition=%wide.region_5.6_spmd, body=%wide.region_4.5_spmd.sunk | while | flops 6 | bytes 143 | solution.py:20
  53.1 40.1 %all-reduce.1 = s32[2048]{0:T(1024)S(1)} all-reduce(s32[2048]{0:T(1024)S(1)} %get-tuple-element.38), channel_id=1, replica_groups=mesh['seq'=32,'head'=4,'rep'=2] {'seq'}, use_global_device_ids=true, to_apply=%add.1 | all-reduce | flops 2048 | bytes 16384
  98.5 12.0 %all_gather.42 = bf16[64,3072]{1,0:T(8,128)(2,1)} all-gather(bf16[64,768]{1,0:T(8,128)(2,1)S(1)} %get-tuple-element.44), channel_id=1, replica_groups=mesh['seq'=32,'head'=4,'rep'=2] {'head'}, dimensions={1}, use_global_device_ids=true | all-gather | bytes 491520 | tf_op jit(solution)/shard_map/all_gather | solution.py:106
  110.6 4.8 copy.35
  115.3 55.7 %all-gather.20.cloned.1.call-done = bf16[1,2048,768]{2,1,0:T(8,128)(2,1)} async-done(((bf16[1,64,768]{2,1,0:T(8,128)(2,1)}), bf16[1,2048,768]{2,1,0:T(8,128)(2,1)}) %all-gather.20.cloned.1.call-update) | async-done | bytes 3145744 | tf_op jit(solution)/shard_map/all_gather | solution.py:57
  171.0 4.7 copy.38
  179.2 75.0 %all-gather.12.cloned.1.call-done = bf16[3072,768]{1,0:T(8,128)(2,1)} async-done(((bf16[96,768]{1,0:T(8,128)(2,1)}), bf16[3072,768]{1,0:T(8,128)(2,1)}) %all-gather.12.cloned.1.call-update) | async-done | bytes 4718608 | tf_op jit(solution)/shard_map/all_gather | solution.py:83
  254.1 4.0 convolution_convert_fusion
  258.2 4.0 multiply_reduce_fusion
  279.7 6.7 %all-to-all-start = ((bf16[64,32,96]{2,0,1:T(8,128)(2,1)}), bf16[64,32,96]{2,0,1:T(8,128)(2,1)}, u32[]{:S(2)}, u32[]{:S(2)}) async-start(bf16[64,32,96]{2,0,1:T(8,128)(2,1)} %copy.58), calls=%async_computation.1 | async-start | bytes 1048576 | tf_op jit(solution)/shard_map/all_to_all | solution.py:109
  288.9 44.2 %all-gather.3 = f32[32,64,6]{1,2,0:T(8,128)S(1)} all-gather(f32[1,64,6]{1,2,0:T(8,128)S(1)} %fusion.62), channel_id=1, replica_groups=mesh['seq'=32,'head'=4,'rep'=2] {'seq'}, dimensions={0}, use_global_device_ids=true | all-gather | bytes 50688 | tf_op jit(solution)/shard_map/all_gather | solution.py:130
  335.4 4.7 copy.46
  340.1 4.8 subtract_exponential_fusion
  344.9 5.6 fusion.33
  350.5 8.2 %reduce-scatter.2.cloned.1.call-done = f32[64,768]{1,0:T(8,128)} async-done(((f32[64,3072]{1,0:T(8,128)}), f32[64,768]{1,0:T(8,128)}) %reduce-scatter.2.cloned.1.call-update) | async-done | bytes 196624 | tf_op jit(solution)/shard_map/reduce_scatter | solution.py:87
  363.3 42.9 %all-gather.4 = f32[32,64,6]{1,2,0:T(8,128)S(1)} all-gather(f32[1,64,6]{1,2,0:T(8,128)S(1)} %bitcast.110), channel_id=1, replica_groups=mesh['seq'=32,'head'=4,'rep'=2] {'seq'}, dimensions={0}, use_global_device_ids=true | all-gather | bytes 50688 | tf_op jit(solution)/shard_map/all_gather | solution.py:131
  410.2 8.1 %psum.14 = f32[1,256]{1,0:T(1,128)} all-reduce(f32[1,256]{1,0:T(1,128)S(1)} %bitcast.114), channel_id=1, replica_groups=mesh['seq'=32,'head'=4,'rep'=2] {'head'}, use_global_device_ids=true, to_apply=%region_10.11 | all-reduce | flops 256 | bytes 2048 | tf_op jit(solution)/shard_map/psum | solution.py:95
  418.3 23.5 %all-gather.14.cloned.1.call-done = bf16[2048,768]{1,0:T(8,128)(2,1)} async-done(((bf16[64,768]{1,0:T(8,128)(2,1)}), bf16[2048,768]{1,0:T(8,128)(2,1)}) %all-gather.14.cloned.1.call-update) | async-done | bytes 3145744 | tf_op jit(solution)/shard_map/all_gather | solution.py:136
  441.9 4.8 copy.50
  446.6 5.3 fusion.32
  455.2 65.8 %all-gather.16.cloned.1.call-done = bf16[2048,768]{1,0:T(8,128)(2,1)} async-done(((bf16[64,768]{1,0:T(8,128)(2,1)}), bf16[2048,768]{1,0:T(8,128)(2,1)}) %all-gather.16.cloned.1.call-update) | async-done | bytes 3145744 | tf_op jit(solution)/shard_map/all_gather | solution.py:113
  528.4 23.0 %all-reduce.4.cloned.1.call-done = f32[96,768]{1,0:T(8,128)} async-done(((f32[96,768]{1,0:T(8,128)}), f32[96,768]{1,0:T(8,128)}) %all-reduce.4.cloned.1.call-update) | async-done | bytes 294928 | tf_op jit(solution)/shard_map/psum | solution.py:116
  (105 shorter events, 66.4 us)
Async XLA Ops:
  7.2 351.5 %copy-start = (bf16[1,256,768]{2,1,0:T(8,128)(2,1)S(1)}, bf16[1,256,768]{2,1,0:T(8,128)(2,1)}, u32[]{:S(2)}) copy-start(bf16[1,256,768]{2,1,0:T(8,128)(2,1)} %param.10) | copy-start | bytes 1179652
  7.2 103.4 %all-gather.18.cloned.1.call-start = ((), (), s32[]{:S(2)}) async-start(), calls=%async_computation.7 | async-start | bytes 3244032 | tf_op jit(solution)/shard_map/all_gather | solution.py:56
  7.9 163.1 %all-gather.20.cloned.1.call-start = ((), (), s32[]{:S(2)}) async-start(), calls=%async_computation.8 | async-start | bytes 3244032 | tf_op jit(solution)/shard_map/all_gather | solution.py:57
  8.7 245.5 %all-gather.12.cloned.1.call-start = ((), (), s32[]{:S(2)}) async-start(), calls=%async_computation.2 | async-start | bytes 4866048 | tf_op jit(solution)/shard_map/all_gather | solution.py:83
  9.4 326.0 %all-gather.22.cloned.1.call-start = ((), (), s32[]{:S(2)}) async-start(), calls=%async_computation.9 | async-start | bytes 3244032 | tf_op jit(solution)/shard_map/all_gather | solution.py:135
  10.0 348.7 %reduce-scatter.2.cloned.1.call-start = ((), (), s32[]{:S(2)}) async-start(), calls=%async_computation.3 | async-start | bytes 983040 | tf_op jit(solution)/shard_map/reduce_scatter | solution.py:87
  11.3 40.6 %copy-start.10 = (pred[256]{0:T(512)(128)(4,1)}, pred[256]{0:T(512)(128)(4,1)S(1)}, u32[]{:S(2)}) copy-start(pred[256]{0:T(512)(128)(4,1)S(1)} %get-tuple-element.40) | copy-start | bytes 772
  11.3 104.0 %copy-start.7 = (s32[256]{0:T(256)}, s32[256]{0:T(256)S(1)}, u32[]{:S(2)}) copy-start(s32[256]{0:T(256)S(1)} %get-tuple-element.41) | copy-start | bytes 3076
  12.5 83.7 %collective-permute-start = (f32[1,768]{1,0:T(1,128)S(1)}, f32[1,768]{1,0:T(1,128)S(1)}, u32[]{:S(2)}, u32[]{:S(2)}) collective-permute-start(f32[1,768]{1,0:T(1,128)S(1)} %broadcast_in_dim.127), channel_id=1, source_target_pairs={{8,0},{16,8},{24,16},{32,24},{40,32},{48,40},{56,48},{64,56},{72,6... | collective-permute-start | bytes 9224 | tf_op jit(solution)/shard_map/ppermute | solution.py:26
  94.6 20.8 %copy-start.9 = (pred[64]{0:T(512)(128)(4,1)}, pred[64]{0:T(512)(128)(4,1)S(1)}, u32[]{:S(2)}) copy-start(pred[64]{0:T(512)(128)(4,1)S(1)} %iota_compare_fusion.6) | copy-start | bytes 196
  96.3 19.1 %copy-start.4 = (f32[768]{0:T(1024)}, f32[768]{0:T(1024)S(1)}, u32[]{:S(2)}) copy-start(f32[768]{0:T(1024)S(1)} %reduce.3) | copy-start | bytes 9220
  258.2 4.6 copy-start.2
  262.1 0.6 copy-start.3
  265.3 176.6 %all-gather.14.cloned.1.call-start = ((), (), s32[]{:S(2)}) async-start(), calls=%async_computation.4 | async-start | bytes 3244032 | tf_op jit(solution)/shard_map/all_gather | solution.py:136
  265.8 255.2 %all-gather.16.cloned.1.call-start = ((), (), s32[]{:S(2)}) async-start(), calls=%async_computation.5 | async-start | bytes 3244032 | tf_op jit(solution)/shard_map/all_gather | solution.py:113
  273.8 12.7 %copy-start.5 = (f32[768]{0:T(1024)S(1)}, f32[768]{0:T(1024)}, u32[]{:S(2)}) copy-start(f32[768]{0:T(1024)} %copy-done.4) | copy-start | bytes 9220
  273.8 12.7 %copy-start.8 = (s32[256]{0:T(256)S(1)}, s32[256]{0:T(256)}, u32[]{:S(2)}) copy-start(s32[256]{0:T(256)} %copy-done.7) | copy-start | bytes 3076
  279.7 175.6 %all-to-all-start = ((bf16[64,32,96]{2,0,1:T(8,128)(2,1)}), bf16[64,32,96]{2,0,1:T(8,128)(2,1)}, u32[]{:S(2)}, u32[]{:S(2)}) async-start(bf16[64,32,96]{2,0,1:T(8,128)(2,1)} %copy.58), calls=%async_computation.1 | async-start | bytes 1048576 | tf_op jit(solution)/shard_map/all_to_all | solution.py:109
  286.4 265.0 %all-reduce.4.cloned.1.call-start = ((), (), s32[]{:S(2)}) async-start(), calls=%async_computation.6 | async-start | bytes 589824 | tf_op jit(solution)/shard_map/psum | solution.py:116
  340.1 4.8 copy-start.6
  344.9 63.9 %copy-start.11 = (pred[256]{0:T(512)(128)(4,1)S(1)}, pred[256]{0:T(512)(128)(4,1)}, u32[]{:S(2)}) copy-start(pred[256]{0:T(512)(128)(4,1)} %copy-done.10) | copy-start | bytes 772
  359.9 48.8 %collective-permute-start.1 = (bf16[1,768]{1,0:T(2,128)(2,1)S(1)}, bf16[1,768]{1,0:T(2,128)(2,1)S(1)}, u32[]{:S(2)}, u32[]{:S(2)}) collective-permute-start(bf16[1,768]{1,0:T(2,128)(2,1)S(1)} %constant_dynamic-slice_fusion), channel_id=1, source_target_pairs={{0,8},{8,16},{16,24},{24,32},{32,40},{40,48},{48,56},{56,64},{64,7... | collective-permute-start | bytes 4616 | tf_op jit(solution)/shard_map/ppermute | solution.py:26
  418.3 28.3 %copy-start.1 = (f32[6,2048,64]{1,2,0:T(8,128)S(1)}, f32[6,2048,64]{1,2,0:T(8,128)}, u32[]{:S(2)}) copy-start(f32[6,2048,64]{1,2,0:T(8,128)} %subtract_exponential_fusion) | copy-start | bytes 9437188
Sparse Core Ops, SparseCore 0:
  10.6 81.3 all-gather.17
  94.6 76.3 all-gather.19
  173.6 80.4 all-gather.11
  256.6 78.4 all-gather.21
  337.5 21.0 reduce-scatter.1
  361.7 80.1 all-gather.13
  444.4 76.5 all-gather.15
  524.6 26.7 all-reduce.3
where the time goes:
time: 564 us; the launch traced here: 560 us
  waiting for transfers between devices  254 us (45%)
  blocking collectives  167 us (30%)
  local copies, waits for them, and re-layouts  48.7 us (9%)
  matrix products  42.8 us (8%)
  between operations  16.1 us (3%)
  starting transfers between devices  14.9 us (3%)
  other arithmetic  10.6 us (2%)
    all_gather x1, waiting for transfers between devices, local(): full_weight = lax.all_gather(out_weight, 'seq', axis=0, tiled=True)  75 us
    all_gather x1, waiting for transfers between devices, local(): lax.all_gather(attended, 'seq', axis=0, tiled=True)  65.8 us
    unnamed x2, blocking collectives  59.8 us
    all_gather x1, waiting for transfers between devices, local(): lax.all_gather(own_values, 'seq', axis=0, tiled=True)  55.7 us
    all_gather x1, blocking collectives, local(): lax.all_gather(log_total, 'seq', axis=0, tiled=True)  44.2 us
    all_gather x1, blocking collectives, local(): lax.all_gather(row_dot, 'seq', axis=0, tiled=True)  42.9 us
    all_gather x1, waiting for transfers between devices, local(): piece_grad = lax.all_gather(out_grad, 'seq', axis=0, tiled=True)  23.5 us
    psum x1, waiting for transfers between devices, local(): weight_grad = lax.psum(window_rows, 'rep')  23 us
  transfers between devices with their start and end apart: 11, of which 6 were waited for; matrix products, arithmetic and copies ran while one was open for 17% of the time, Pallas kernels for 0%

commit v1 on v0

v1 whole, which is shorter than its diff:
```python
import jax
import jax.numpy as jnp
from jax import lax
from jax.experimental import pallas as pl
from jax.experimental.pallas import tpu as pltpu
from jax.sharding import PartitionSpec as P

MESH = pl.DeviceIdType.MESH
F32, BF16 = jnp.float32, jnp.bfloat16

HEAD_DIM = 128
NS = 32
NH = 6
D = 768
CAP = 64
NB = 256
SCALE = HEAD_DIM ** -0.5
SCALE_LOG2E = SCALE * 1.4426950408889634
FAR_QUERY = 4096.0
FAR_KEY = 8192.0


def att_seq(h, w):
    return lax.div((2 * h + w) * 8, 3)


def nt(a, b):
    return lax.dot_general(a, b, (((1,), (1,)), ((), ())), preferred_element_type=F32)


def nn(a, b):
    return jnp.dot(a, b, preferred_element_type=F32)


def kernel(
    states, starts, conf, q_in, k_in, v_in, w_in, up,
    byte_grad, conf_grad, dq_out, dk_out, dv_out, wg_out,
    stage, kv, qb, wq, gext, spill_in, g_bf, gq, dop, dob,
    kt, vt, kkb, probs, inv, a_out, ab, pp, pr, wgp, wgr, wsum, wsib,
    lrow, prow, cpart, call, dqb, acc, sib, dkf, sel_s, grows,
    kv_send, kv_recv, q_send, q_recv, w_send, w_recv, sp_send, sp_recv, g_send, g_recv,
    do_send, do_recv, a_send, a_recv, p_send, p_recv, wg_send, wg_recv, ws_send, ws_recv,
    lr_send, lr_recv, c_send, c_recv, dq_send, dq_recv, dk_send, dk_recv, dv_send, dv_recv,
    ex_send, ex_recv,
):
    s = lax.axis_index("seq")
    x = lax.axis_index("head")
    r = lax.axis_index("rep")
    q = lax.div(s, 8)
    m = lax.rem(s, 8)
    half = lax.div(q, 2)
    sub = lax.rem(q, 2)
    att = lax.div(3 * s + 7, 8)
    is_att = jnp.logical_and(lax.div(att * 8, 3) == s, att < 12)
    att_h = lax.div(att, 2)
    att_w = lax.rem(att, 2)

    def same(t):
        return jnp.logical_and(jnp.logical_and(t[0] == s, t[1] == x), t[2] == r)

    def send(src, dst, ssem, rsem, t):
        mine = same(t)

        @pl.when(jnp.logical_not(mine))
        def _():
            pltpu.make_async_remote_copy(src, dst, ssem, rsem, device_id=t, device_id_type=MESH).start()

        @pl.when(mine)
        def _():
            pltpu.make_async_copy(src, dst, rsem).start()

    def sent(src, dst, ssem, rsem, t):
        @pl.when(jnp.logical_not(same(t)))
        def _():
            pltpu.make_async_remote_copy(src, dst, ssem, rsem, device_id=t, device_id_type=MESH).wait_send()

    def landed(ref, rsem):
        pltpu.make_async_copy(ref, ref, rsem).wait()

    def lanes(h):
        return pl.ds(h * HEAD_DIM if isinstance(h, int) else pl.multiple_of(h * HEAD_DIM, HEAD_DIM), HEAD_DIM)

    def kv_flow(op):
        for h in range(NH):
            for c in range(2):
                op(stage.at[h], kv.at[s], kv_send.at[2 * h + c], kv_recv, (att_seq(h, r), x, c))

    def q_flow(op):
        for h in range(NH):
            op(q_in.at[0, :, lanes(h)], qb.at[m, sub], q_send.at[h], q_recv, (att_seq(h, r), x, half))

    def w_flow(op):
        for i in range(1, 8):
            op(w_in, wq.at[m], w_send.at[i - 1], w_recv, (8 * q + lax.rem(m + i, 8), x, r))

    def g_flow(op):
        for i in range(4):
            op(g_bf, gq.at[q], g_send.at[i], g_recv, (8 * x + m, i, r))

    def do_flow(op):
        for h in range(NH):
            for c in range(2):
                op(dop.at[pl.ds(2 * c, 2), :, lanes(h)], dob.at[q, m], do_send.at[2 * h + c], do_recv,
                   (att_seq(h, r), x, c))

    def a_flow(op, mm):
        for i in range(4):
            op(a_out.at[mm], ab.at[pl.ds(2 * r, 2), :, lanes(att_h)], a_send.at[mm * 4 + i], a_recv,
               (8 * i + mm, x, att_w))

    def p_flow(op):
        for k in range(4):
            op(pp.at[k], pr.at[x], p_send.at[k], p_recv, (8 * k + m, q, r))

    def wg_flow(op):
        for i in range(1, 8):
            t = lax.rem(m + i, 8)
            op(wgp.at[t], wgr.at[m], wg_send.at[i - 1], wg_recv, (8 * q + t, x, r))

    def c_flow(op):
        for i in range(1, 4):
            op(cpart, call.at[x], c_send.at[i - 1], c_recv, (s, lax.rem(x + i, 4), r))

    def dq_flow(op, mm):
        for k in range(2):
            op(dqb.at[mm, k], dq_out.at[0, :, lanes(att_h)], dq_send.at[mm * 2 + k], dq_recv,
               (8 * (2 * r + k) + mm, x, att_w))

    def dkv_flow(op, j):
        op(dkf.at[0, j], dk_out.at[0, :, lanes(att_h)], dk_send.at[j], dk_recv, (16 * r + j, x, att_w))
        op(dkf.at[1, j], dv_out.at[0, :, lanes(att_h)], dv_send.at[j], dv_recv, (16 * r + j, x, att_w))

    def remote(src, dst, ssem, rsem, t):
        return pltpu.make_async_remote_copy(src, dst, ssem, rsem, device_id=t, device_id_type=MESH)

    spill_copy = remote(gext.at[pl.ds(64, 8)], spill_in, sp_send, sp_recv, (s - 1, x, r))
    row_copy = remote(lrow, prow, lr_send, lr_recv, (s + 1, x, r))
    sib_id = (s, x, 1 - r)
    wsum_copy = remote(wsum, wsib, ws_send, ws_recv, sib_id)
    ex_copy = remote(acc.at[1 - r], sib, ex_send, ex_recv, sib_id)

    barrier = pltpu.get_barrier_semaphore()

    def greet(t):
        @pl.when(jnp.logical_not(same(t)))
        def _():
            pl.semaphore_signal(barrier, inc=1, device_id=t, device_id_type=MESH)

    for h in range(NH):
        for c in range(2):
            greet((att_seq(h, r), x, c))
    for i in range(1, 8):
        greet((8 * q + lax.rem(m + i, 8), x, r))
    for k in range(4):
        for i in range(4):
            greet((8 * k + m, i, r))
    greet(sib_id)

    @pl.when(s > 0)
    def _():
        greet((s - 1, x, r))

    @pl.when(s < NS - 1)
    def _():
        greet((s + 1, x, r))

    @pl.when(is_att)
    def _():
        def one(j, _):
            greet((j, x, att_w))
            return 0

        lax.fori_loop(0, NS, one, 0)

    start_row = starts[...].astype(F32)
    before = lax.broadcasted_iota(jnp.int32, (NB, NB), 0) <= lax.broadcasted_iota(jnp.int32, (NB, NB), 1)
    tri = jnp.where(before, 1.0, 0.0).astype(BF16)
    rank = nn(jnp.broadcast_to(start_row, (16, NB)).astype(BF16), tri)[0:1] - 1.0
    count = jnp.sum(start_row, axis=1, keepdims=True)
    for h in range(NH):
        cols = slice(h * HEAD_DIM, (h + 1) * HEAD_DIM)
        stage[h, 0:64] = k_in[0, :, cols]
        stage[h, 64:128] = v_in[0, :, cols]
        stage[h, 128:144] = jnp.broadcast_to(count, (16, HEAD_DIM)).astype(BF16)
    slot80 = lax.broadcasted_iota(jnp.int32, (80, NB), 0).astype(F32)
    want = jnp.where(slot80 < 64.0, slot80, jnp.where(slot80 == 64.0, -1.0, -2.0))
    sel = jnp.where(jnp.broadcast_to(rank, (80, NB)) == want, 1.0, 0.0)
    sel_s[...] = sel

    partners = (
        12 + 7 + 15 + 1
        + jnp.where(s > 0, 1, 0) + jnp.where(s < NS - 1, 1, 0)
        + jnp.where(is_att, jnp.where(att_w == r, 30, 32), 0)
    )
    pl.semaphore_wait(barrier, partners)

    kv_flow(send)
    q_flow(send)
    w_flow(lambda *a: remote(*a).start())
    wq[m] = w_in[...]

    weight = sel * conf[...]
    w_hi = weight.astype(BF16)
    w_lo = (weight - w_hi.astype(F32)).astype(BF16)
    upstream = up[0]
    gext[...] = nn(w_hi, upstream) + nn(w_lo, upstream)

    @pl.when(s > 0)
    def _():
        spill_copy.start()

    @pl.when(s == NS - 1)
    def _():
        spill_in[...] = jnp.zeros_like(spill_in)

    @pl.when(s == 0)
    def _():
        prow[...] = jnp.zeros_like(prow)

    picked = sel[0:64] * start_row
    picked_t = picked.T.astype(BF16)
    grows[...] = nn(picked.astype(BF16), states[0])

    @pl.when(s < NS - 1)
    def _():
        spill_copy.wait_recv()

    last = lax.broadcasted_iota(jnp.int32, (64, D), 0).astype(F32) == count - 1.0
    group_grad = gext[0:64] + jnp.where(last, spill_in[0:1], 0.0)
    g_hi = group_grad.astype(BF16)
    g_bf[...] = g_hi
    g_flow(send)
    g_lo = (group_grad - g_hi.astype(F32)).astype(BF16)
    byte_grad[0] = (upstream.astype(F32) + nn(picked_t, g_hi) + nn(picked_t, g_lo)).astype(BF16)

    @pl.when(is_att)
    def _():
        landed(kv, kv_recv)
        landed(qb, q_recv)
        kt[...] = kv[:, 0:64, :].reshape(2048, HEAD_DIM).T
        vt[...] = kv[:, 64:128, :].reshape(2048, HEAD_DIM).T
        lane = lax.broadcasted_iota(jnp.int32, (1, 128), 1).astype(F32)
        for p in range(16):
            c0 = kv[2 * p, 128:144, :].astype(F32)[0:1]
            c1 = kv[2 * p + 1, 128:144, :].astype(F32)[0:1]
            live = jnp.where(lane < 64.0, jnp.where(lane < c0, 1.0, 0.0), jnp.where(lane - 64.0 < c1, 1.0, 0.0))
            row = jnp.where(live > 0.0, lane + 128.0 * p, FAR_KEY)
            kkb[:, p * 128:(p + 1) * 128] = jnp.broadcast_to(row, (8, 128))

        def forward(i, _):
            queries = qb[pl.ds(2 * i, 2)].reshape(256, HEAD_DIM)
            slot = lax.broadcasted_iota(jnp.int32, (64, 128), 0).astype(F32)
            places = []
            for mm in range(2):
                for k in range(2):
                    block = 8 * (2 * r + k) + 2 * i + mm
                    cnt = kv[block, 128:144, :].astype(F32)[0:1]
                    base = (block * 64).astype(F32)
                    places.append(jnp.where(slot < cnt, slot + base, FAR_QUERY))
            place = jnp.concatenate(places, axis=0)
            place = jnp.concatenate([place] * 16, axis=1)
            scores = nn(queries, kt[...])
            scores = jnp.where(jnp.broadcast_to(kkb[0:1], (256, 2048)) <= place, scores, -jnp.inf)
            top = jnp.max(scores, axis=1, keepdims=True)
            attention = jnp.exp2((scores - top) * SCALE_LOG2E)
            total = jnp.sum(attention, axis=1, keepdims=True)
            rounded = attention.astype(BF16)
            probs[i] = rounded
            inverse = 1.0 / total
            inv[i] = jnp.broadcast_to(inverse, (256, HEAD_DIM))
            out = nn(rounded, kv[:, 64:128, :].reshape(2048, HEAD_DIM)) * inverse
            a_out[pl.ds(2 * i, 2)] = out.astype(BF16).reshape(2, 2, 64, HEAD_DIM)
            a_flow(send, 2 * i)
            a_flow(send, 2 * i + 1)
            return 0

        lax.fori_loop(0, 4, forward, 0)

    landed(wq.at[pl.ds(0, 7)], w_recv)
    landed(gq, g_recv)
    g_all = gq[...].reshape(256, D)
    w_all = wq[...].reshape(D, D)
    dop[...] = nn(g_all, w_all).astype(BF16).reshape(4, 64, D)
    do_flow(send)

    landed(ab, a_recv)
    a_all = ab[...].reshape(256, D)
    pp[...] = nt(a_all, w_all).astype(BF16).reshape(4, 64, D)
    p_flow(send)
    wgp[...] = nn(g_all.T, a_all).astype(BF16).reshape(8, 96, D)
    wg_flow(lambda *a: remote(*a).start())

    @pl.when(is_att)
    def _():
        landed(dob, do_recv)
        acc[...] = jnp.zeros_like(acc)

        def backward(i, _):
            queries = qb[pl.ds(2 * i, 2)].reshape(256, HEAD_DIM)
            grad = dob[0, pl.ds(2 * i, 2)].astype(F32)
            for j in range(1, 4):
                grad = grad + dob[j, pl.ds(2 * i, 2)].astype(F32)
            grad = grad.reshape(256, HEAD_DIM).astype(BF16).astype(F32)
            grad = (grad * inv[i]).astype(BF16)
            attended = a_out[pl.ds(2 * i, 2)].reshape(256, HEAD_DIM)
            dots = jnp.sum(grad.astype(F32) * attended.astype(F32), axis=1, keepdims=True)
            flow = nn(grad, vt[...])
            weights = probs[i]
            dscore = (weights.astype(F32) * (flow - dots)).astype(BF16)
            dq = nn(dscore, kv[:, 0:64, :].reshape(2048, HEAD_DIM)) * SCALE
            dqb[pl.ds(2 * i, 2)] = dq.astype(BF16).reshape(2, 2, 64, HEAD_DIM)
            dq_flow(send, 2 * i)
            dq_flow(send, 2 * i + 1)
            dk = nn(queries.T, dscore)
            dv = nn(grad.T, weights)
            for c in range(2):
                cols = slice(1024 * c, 1024 * (c + 1))
                acc[c, 0] += dk[:, cols]
                acc[c, 1] += dv[:, cols]
            return 0

        lax.fori_loop(0, 4, backward, 0)
        ex_copy.start()
        ex_copy.wait_recv()
        dkf[0] = ((acc[r, 0] + sib[0]) * SCALE).T.astype(BF16).reshape(16, 64, HEAD_DIM)
        dkf[1] = (acc[r, 1] + sib[1]).T.astype(BF16).reshape(16, 64, HEAD_DIM)

        def out(j, _):
            dkv_flow(send, j)
            return 0

        lax.fori_loop(0, 16, out, 0)

    landed(pr, p_recv)
    total = grows[...]
    for i in range(4):
        total = total + pr[i].astype(F32)
    group_out = total.astype(BF16)
    lrow[...] = jnp.broadcast_to(
        jnp.sum(jnp.where(last, group_out.astype(F32), 0.0), axis=0, keepdims=True), (16, D)
    ).astype(BF16)

    @pl.when(s < NS - 1)
    def _():
        row_copy.start()

    landed(wgr.at[pl.ds(0, 7)], wg_recv)
    wgr[m] = wgp[m]
    total_w = wgr[0].astype(F32)
    for i in range(1, 8):
        total_w = total_w + wgr[i].astype(F32)
    wsum[...] = total_w
    wsum_copy.start()

    @pl.when(s > 0)
    def _():
        row_copy.wait_recv()

    rows = jnp.concatenate([group_out, prow[...]], axis=0)
    cross = nt(rows, up[0])
    part = jnp.sum(sel_s[...] * cross, axis=0, keepdims=True)
    cpart[...] = jnp.broadcast_to(part, (8, NB))
    call[x] = cpart[...]
    c_flow(lambda *a: remote(*a).start())

    wsum_copy.wait_recv()
    wg_out[...] = wsum[...] + wsib[...]
    landed(call.at[pl.ds(0, 3)], c_recv)
    conf_grad[...] = (call[0] + call[1] + call[2] + call[3])[0:1]

    kv_flow(sent)
    q_flow(sent)
    w_flow(sent)
    g_flow(sent)
    do_flow(sent)
    p_flow(sent)
    wg_flow(sent)
    c_flow(sent)
    wsum_copy.wait_send()

    @pl.when(s > 0)
    def _():
        spill_copy.wait_send()

    @pl.when(s < NS - 1)
    def _():
        row_copy.wait_send()

    @pl.when(is_att)
    def _():
        ex_copy.wait_send()

        def one(j, _):
            a_flow(sent, j)
            dq_flow(sent, j)
            return 0

        lax.fori_loop(0, 8, one, 0)

        def two(j, _):
            dkv_flow(sent, j)
            return 0

        lax.fori_loop(0, 16, two, 0)

    landed(dq_out, dq_recv)
    landed(dk_out, dk_recv)
    landed(dv_out, dv_recv)


def local(byte_states, boundary, confidence, query_rows, key_rows, value_rows, out_weight, upstream):
    vmem = pl.BlockSpec(memory_space=pltpu.VMEM)
    dma = pltpu.SemaphoreType.DMA
    rows = jax.ShapeDtypeStruct((1, CAP, D), BF16)
    return pl.pallas_call(
        kernel,
        out_shape=(
            jax.ShapeDtypeStruct((1, NB, D), BF16),
            jax.ShapeDtypeStruct((1, NB), F32),
            rows, rows, rows,
            jax.ShapeDtypeStruct((96, D), F32),
        ),
        in_specs=[vmem] * 8,
        out_specs=(vmem,) * 6,
        scratch_shapes=[
            pltpu.VMEM((NH, 144, 128), BF16),
            pltpu.VMEM((NS, 144, 128), BF16),
            pltpu.VMEM((8, 2, 64, 128), BF16),
            pltpu.VMEM((8, 96, D), BF16),
            pltpu.VMEM((80, D), F32),
            pltpu.VMEM((8, D), F32),
            pltpu.VMEM((64, D), BF16),
            pltpu.VMEM((4, 64, D), BF16),
            pltpu.VMEM((4, 64, D), BF16),
            pltpu.VMEM((4, 8, 2, 64, 128), BF16),
            pltpu.VMEM((128, 2048), BF16),
            pltpu.VMEM((128, 2048), BF16),
            pltpu.VMEM((8, 2048), F32),
            pltpu.VMEM((4, 256, 2048), BF16),
            pltpu.VMEM((4, 256, 128), F32),
            pltpu.VMEM((8, 2, 64, 128), BF16),
            pltpu.VMEM((4, 64, D), BF16),
            pltpu.VMEM((4, 64, D), BF16),
            pltpu.VMEM((4, 64, D), BF16),
            pltpu.VMEM((8, 96, D), BF16),
            pltpu.VMEM((8, 96, D), BF16),
            pltpu.VMEM((96, D), F32),
            pltpu.VMEM((96, D), F32),
            pltpu.VMEM((16, D), BF16),
            pltpu.VMEM((16, D), BF16),
            pltpu.VMEM((8, NB), F32),
            pltpu.VMEM((4, 8, NB), F32),
            pltpu.VMEM((8, 2, 64, 128), BF16),
            pltpu.VMEM((2, 2, 128, 1024), F32),
            pltpu.VMEM((2, 128, 1024), F32),
            pltpu.VMEM((2, 16, 64, 128), BF16),
            pltpu.VMEM((80, NB), F32),
            pltpu.VMEM((64, D), F32),
            dma((12,)), dma,
            dma((6,)), dma,
            dma((7,)), dma,
            dma, dma,
            dma((4,)), dma,
            dma((12,)), dma,
            dma((32,)), dma,
            dma((4,)), dma,
            dma((7,)), dma,
            dma, dma,
            dma, dma,
            dma((3,)), dma,
            dma((16,)), dma,
            dma((16,)), dma,
            dma((16,)), dma,
            dma, dma,
        ],
        compiler_params=pltpu.CompilerParams(
            collective_id=0, has_side_effects=True, vmem_limit_bytes=56 * 1024 * 1024
        ),
        cost_estimate=pl.CostEstimate(flops=8_000_000_000, bytes_accessed=20_000_000, transcendentals=3_000_000),
    )(byte_states, boundary, confidence, query_rows, key_rows, value_rows, out_weight, upstream)


def solution(mesh):
    split = P("rep", "seq", "head")
    bytes_ = P("rep", "seq")
    return jax.shard_map(
        local,
        mesh=mesh,
        in_specs=(split, bytes_, bytes_, split, split, split, P("seq", "head"), split),
        out_specs=(split, bytes_, split, split, split, P("seq", "head")),
        check_vma=False,
    )
```

time: 564 us -> 130 us (0.23)
  the two profiles are of different devices: /device:TPU:68 before, /device:TPU:24 now
where the time goes in v1:
time: 130 us
  Pallas kernels  124 us (95%)
  local copies, waits for them, and re-layouts  5.03 us (4%)
    pallas_call x1, Pallas kernels, local(): pl.pallas_call(kernel, out_shape=(jax.ShapeDtypeStruct((1, NB, D), BF16),...  124 us
    unnamed x16, local copies, waits for them, and re-layouts  5.03 us

profile of v1, /device:TPU:24, one launch (start us, length us, event | category | flops | bytes accessed | tf_op | source)
XLA Modules:
  0.0 129.6 jit_solution(4624655438221955425)
XLA Ops:
  0.6 123.9 %shard_map.127 = (bf16[1,256,768]{2,1,0:T(8,128)(2,1)}, f32[1,256]{1,0:T(1,128)}, bf16[1,64,768]{2,1,0:T(8,128)(2,1)}, bf16[1,64,768]{2,1,0:T(8,128)(2,1)}, bf16...) custom-call(bf16[1,256,768]{2,1,0:T(8,128)(2,1)} %states.1, s32[1,256]{1,0:T(1,128)} %starts.1, f32[1,256]{1,0:T(1,128)} %conf.1, ...), custom_call_target="tpu_custom_call" | custom-call | flops 8000000000 | bytes 20000000 | tf_op jit(solution)/shard_map/pallas_call | solution.py:415
  124.6 0.0 copy-start.4
  124.6 0.0 copy-start.3
  124.6 0.0 copy-start.2
  124.6 0.0 copy-start.1
  124.6 1.8 %copy.20 = bf16[1,256,768]{2,1,0:T(8,128)(2,1)} copy(bf16[1,256,768]{2,1,0:T(8,128)(2,1)} %get-tuple-element.12) | data formatting | bytes 786432
  126.4 0.0 copy-done.4
  126.4 0.6 copy.21
  127.0 0.0 copy-done.3
  127.0 0.0 copy-start
  127.0 0.6 copy.22
  127.6 0.0 copy-done.2
  127.6 0.6 copy.23
  128.3 0.0 copy-done.1
  128.3 0.6 copy.24
  128.9 0.0 copy-done
  128.9 0.7 copy.25
Async XLA Ops:
  124.6 1.9 %copy-start.4 = (f32[1,256]{1,0:T(1,128)S(1)}, f32[1,256]{1,0:T(1,128)}, u32[]{:S(2)}) copy-start(f32[1,256]{1,0:T(1,128)} %get-tuple-element.13) | copy-start | bytes 3076
  124.6 2.4 %copy-start.3 = (bf16[1,64,768]{2,1,0:T(8,128)(2,1)S(1)}, bf16[1,64,768]{2,1,0:T(8,128)(2,1)}, u32[]{:S(2)}) copy-start(bf16[1,64,768]{2,1,0:T(8,128)(2,1)} %get-tuple-element.14) | copy-start | bytes 294916
  124.6 3.0 %copy-start.2 = (bf16[1,64,768]{2,1,0:T(8,128)(2,1)S(1)}, bf16[1,64,768]{2,1,0:T(8,128)(2,1)}, u32[]{:S(2)}) copy-start(bf16[1,64,768]{2,1,0:T(8,128)(2,1)} %get-tuple-element.15) | copy-start | bytes 294916
  124.6 3.7 %copy-start.1 = (bf16[1,64,768]{2,1,0:T(8,128)(2,1)S(1)}, bf16[1,64,768]{2,1,0:T(8,128)(2,1)}, u32[]{:S(2)}) copy-start(bf16[1,64,768]{2,1,0:T(8,128)(2,1)} %get-tuple-element.16) | copy-start | bytes 294916
  127.0 1.9 %copy-start = (f32[96,768]{1,0:T(8,128)S(1)}, f32[96,768]{1,0:T(8,128)}, u32[]{:S(2)}) copy-start(f32[96,768]{1,0:T(8,128)} %get-tuple-element.17) | copy-start | bytes 884740

commit v2 on v1

--- a/solution.py
+++ b/solution.py
@@ -35,11 +35,13 @@
 def kernel(
     states, starts, conf, q_in, k_in, v_in, w_in, up,
     byte_grad, conf_grad, dq_out, dk_out, dv_out, wg_out,
-    stage, kv, qb, wq, gext, spill_in, g_bf, gq, dop, dob,
-    kt, vt, kkb, probs, inv, a_out, ab, pp, pr, wgp, wgr, wsum, wsib,
+    stage, kv, wq, gext, spill_in, g_bf, gq, dop, dob,
+    kt, vt, kkb, probs, inv, a_out, ab, pp, p1, ps, pr, wgp, wgs, wg0, wh, wg1, wt, wg2, wsum,
     lrow, prow, cpart, call, dqb, acc, sib, dkf, sel_s, grows,
-    kv_send, kv_recv, q_send, q_recv, w_send, w_recv, sp_send, sp_recv, g_send, g_recv,
-    do_send, do_recv, a_send, a_recv, p_send, p_recv, wg_send, wg_recv, ws_send, ws_recv,
+    kv_send, kv_recv, fw_send, fw_recv, wa_send, wa_recv, wb_send, wb_recv, wc_send, wc_recv, wd_send, wd_recv,
+    sp_send, sp_recv, g_send, g_recv, gx_send, gx_recv,
+    do_send, do_recv, a_send, a_recv, px_send, px_recv, p_send, p_recv,
+    w0_send, w0_recv, w1_send, w1_recv, w2_send, w2_recv, ws_send, ws_recv,
     lr_send, lr_recv, c_send, c_recv, dq_send, dq_recv, dk_send, dk_recv, dv_send, dv_recv,
     ex_send, ex_recv,
 ):
@@ -48,8 +50,9 @@
     r = lax.axis_index("rep")
     q = lax.div(s, 8)
     m = lax.rem(s, 8)
+    zp = lax.div(m, 4)
+    y = lax.rem(m, 4)
     half = lax.div(q, 2)
-    sub = lax.rem(q, 2)
     att = lax.div(3 * s + 7, 8)
     is_att = jnp.logical_and(lax.div(att * 8, 3) == s, att < 12)
     att_h = lax.div(att, 2)
@@ -77,25 +80,54 @@
     def landed(ref, rsem):
         pltpu.make_async_copy(ref, ref, rsem).wait()
 
+    def remote(src, dst, ssem, rsem, t):
+        return pltpu.make_async_remote_copy(src, dst, ssem, rsem, device_id=t, device_id_type=MESH)
+
+    def start(*a):
+        remote(*a).start()
+
+    def finish(*a):
+        remote(*a).wait_send()
+
     def lanes(h):
         return pl.ds(h * HEAD_DIM if isinstance(h, int) else pl.multiple_of(h * HEAD_DIM, HEAD_DIM), HEAD_DIM)
 
+    mine48 = pl.ds(pl.multiple_of(48 * r, 16), 48)
+    z_peer = (s + 4 - 8 * zp, x, r)
+    sib_id = (s, x, 1 - r)
+
+    def y_peer(i):
+        return (s - y + lax.rem(y + i, 4), x, r)
+
+    def x_peer(i):
+        return (s, lax.rem(x + i, 4), r)
+
     def kv_flow(op):
         for h in range(NH):
-            for c in range(2):
-                op(stage.at[h], kv.at[s], kv_send.at[2 * h + c], kv_recv, (att_seq(h, r), x, c))
-
-    def q_flow(op):
-        for h in range(NH):
-            op(q_in.at[0, :, lanes(h)], qb.at[m, sub], q_send.at[h], q_recv, (att_seq(h, r), x, half))
-
-    def w_flow(op):
-        for i in range(1, 8):
-            op(w_in, wq.at[m], w_send.at[i - 1], w_recv, (8 * q + lax.rem(m + i, 8), x, r))
+            op(stage.at[h], kv.at[s], kv_send.at[h], kv_recv, (att_seq(h, r), x, half))
+
+    def wa_flow(op):
+        op(w_in.at[mine48], wq.at[zp, y, mine48], wa_send, wa_recv, z_peer)
+
+    def wb_flow(op):
+        for i in range(1, 4):
+            op(w_in.at[mine48], wq.at[zp, y, mine48], wb_send.at[i - 1], wb_recv, y_peer(i))
+
+    def wc_flow(op):
+        for i in range(1, 4):
+            op(wq.at[1 - zp, y, mine48], wq.at[1 - zp, y, mine48], wc_send.at[i - 1], wc_recv, y_peer(i))
+
+    def wd_flow(op):
+        op(wq.at[:, :, mine48], wq.at[:, :, mine48], wd_send, wd_recv, sib_id)
+
+    turned = (8 * x + m, q, r)
 
     def g_flow(op):
-        for i in range(4):
-            op(g_bf, gq.at[q], g_send.at[i], g_recv, (8 * x + m, i, r))
+        op(g_bf, gq.at[q], g_send, g_recv, turned)
+
+    def gx_flow(op):
+        for i in range(1, 4):
+            op(gq.at[x], gq.at[x], gx_send.at[i - 1], gx_recv, x_peer(i))
 
     def do_flow(op):
         for h in range(NH):
@@ -108,18 +140,29 @@
             op(a_out.at[mm], ab.at[pl.ds(2 * r, 2), :, lanes(att_h)], a_send.at[mm * 4 + i], a_recv,
                (8 * i + mm, x, att_w))
 
+    def px_flow(op):
+        for i in range(1, 4):
+            op(pp.at[lax.rem(x + i, 4)], p1.at[x], px_send.at[i - 1], px_recv, x_peer(i))
+
     def p_flow(op):
-        for k in range(4):
-            op(pp.at[k], pr.at[x], p_send.at[k], p_recv, (8 * k + m, q, r))
-
-    def wg_flow(op):
-        for i in range(1, 8):
-            t = lax.rem(m + i, 8)
-            op(wgp.at[t], wgr.at[m], wg_send.at[i - 1], wg_recv, (8 * q + t, x, r))
+        op(ps, pr, p_send, p_recv, turned)
+
+    def w0_flow(op):
+        op(wgs, wg0, w0_send, w0_recv, sib_id)
+
+    def w1_flow(op):
+        for i in range(1, 4):
+            op(wh.at[:, lax.rem(y + i, 4)], wg1.at[y], w1_send.at[i - 1], w1_recv, y_peer(i))
+
+    def w2_flow(op):
+        op(wt.at[1 - zp], wg2, w2_send, w2_recv, z_peer)
+
+    def ws_flow(op):
+        op(wsum, wg_out.at[mine48], ws_send, ws_recv, sib_id)
 
     def c_flow(op):
         for i in range(1, 4):
-            op(cpart, call.at[x], c_send.at[i - 1], c_recv, (s, lax.rem(x + i, 4), r))
+            op(cpart, call.at[x], c_send.at[i - 1], c_recv, x_peer(i))
 
     def dq_flow(op, mm):
         for k in range(2):
@@ -130,13 +173,12 @@
         op(dkf.at[0, j], dk_out.at[0, :, lanes(att_h)], dk_send.at[j], dk_recv, (16 * r + j, x, att_w))
         op(dkf.at[1, j], dv_out.at[0, :, lanes(att_h)], dv_send.at[j], dv_recv, (16 * r + j, x, att_w))
 
-    def remote(src, dst, ssem, rsem, t):
-        return pltpu.make_async_remote_copy(src, dst, ssem, rsem, device_id=t, device_id_type=MESH)
+    def fw_flow(op):
+        part = kv.at[pl.ds(16 * r, 16), pl.ds(0, 144)]
+        op(part, part, fw_send, fw_recv, sib_id)
 
     spill_copy = remote(gext.at[pl.ds(64, 8)], spill_in, sp_send, sp_recv, (s - 1, x, r))
     row_copy = remote(lrow, prow, lr_send, lr_recv, (s + 1, x, r))
-    sib_id = (s, x, 1 - r)
-    wsum_copy = remote(wsum, wsib, ws_send, ws_recv, sib_id)
     ex_copy = remote(acc.at[1 - r], sib, ex_send, ex_recv, sib_id)
 
     barrier = pltpu.get_barrier_semaphore()
@@ -149,11 +191,11 @@
     for h in range(NH):
         for c in range(2):
             greet((att_seq(h, r), x, c))
-    for i in range(1, 8):
-        greet((8 * q + lax.rem(m + i, 8), x, r))
-    for k in range(4):
-        for i in range(4):
-            greet((8 * k + m, i, r))
+    for i in range(1, 4):
+        greet(y_peer(i))
+        greet(x_peer(i))
+    greet(z_peer)
+    greet(turned)
     greet(sib_id)
 
     @pl.when(s > 0)
@@ -177,49 +219,49 @@
     tri = jnp.where(before, 1.0, 0.0).astype(BF16)
     rank = nn(jnp.broadcast_to(start_row, (16, NB)).astype(BF16), tri)[0:1] - 1.0
     count = jnp.sum(start_row, axis=1, keepdims=True)
+    slot80 = lax.broadcasted_iota(jnp.int32, (80, NB), 0).astype(F32)
+    want = jnp.where(slot80 < 64.0, slot80, jnp.where(slot80 == 64.0, -1.0, -2.0))
+    sel = jnp.where(jnp.broadcast_to(rank, (80, NB)) == want, 1.0, 0.0)
+    sel_s[...] = sel
+    weight = sel * conf[...]
+    w_hi = weight.astype(BF16)
+    w_lo = (weight - w_hi.astype(F32)).astype(BF16)
+    upstream = up[0]
+    gext[...] = nn(w_hi, upstream) + nn(w_lo, upstream)
     for h in range(NH):
         cols = slice(h * HEAD_DIM, (h + 1) * HEAD_DIM)
         stage[h, 0:64] = k_in[0, :, cols]
         stage[h, 64:128] = v_in[0, :, cols]
         stage[h, 128:144] = jnp.broadcast_to(count, (16, HEAD_DIM)).astype(BF16)
-    slot80 = lax.broadcasted_iota(jnp.int32, (80, NB), 0).astype(F32)
-    want = jnp.where(slot80 < 64.0, slot80, jnp.where(slot80 == 64.0, -1.0, -2.0))
-    sel = jnp.where(jnp.broadcast_to(rank, (80, NB)) == want, 1.0, 0.0)
-    sel_s[...] = sel
+        stage[h, 144:208] = q_in[0, :, cols]
+    picked = sel[0:64] * start_row
+    picked_t = picked.T.astype(BF16)
+    grows[...] = nn(picked.astype(BF16), states[0])
+    wq[zp, y, mine48] = w_in[mine48]
+
+    @pl.when(s == NS - 1)
+    def _():
+        spill_in[...] = jnp.zeros_like(spill_in)
+
+    @pl.when(s == 0)
+    def _():
+        prow[...] = jnp.zeros_like(prow)
 
     partners = (
-        12 + 7 + 15 + 1
+        12 + 3 + 3 + 1 + 1
+        + jnp.where(q == x, 0, 1)
         + jnp.where(s > 0, 1, 0) + jnp.where(s < NS - 1, 1, 0)
         + jnp.where(is_att, jnp.where(att_w == r, 30, 32), 0)
     )
     pl.semaphore_wait(barrier, partners)
 
+    @pl.when(s > 0)
+    def _():
+        spill_copy.start()
+
+    wa_flow(start)
     kv_flow(send)
-    q_flow(send)
-    w_flow(lambda *a: remote(*a).start())
-    wq[m] = w_in[...]
-
-    weight = sel * conf[...]
-    w_hi = weight.astype(BF16)
-    w_lo = (weight - w_hi.astype(F32)).astype(BF16)
-    upstream = up[0]
-    gext[...] = nn(w_hi, upstream) + nn(w_lo, upstream)
-
-    @pl.when(s > 0)
-    def _():
-        spill_copy.start()
-
-    @pl.when(s == NS - 1)
-    def _():
-        spill_in[...] = jnp.zeros_like(spill_in)
-
-    @pl.when(s == 0)
-    def _():
-        prow[...] = jnp.zeros_like(prow)
-
-    picked = sel[0:64] * start_row
-    picked_t = picked.T.astype(BF16)
-    grows[...] = nn(picked.astype(BF16), states[0])
+    wb_flow(start)
 
     @pl.when(s < NS - 1)
     def _():
@@ -230,13 +272,32 @@
     g_hi = group_grad.astype(BF16)
     g_bf[...] = g_hi
     g_flow(send)
+    landed(w_in.at[pl.ds(0, 48)], wa_recv)
+    wc_flow(start)
+    landed(g_bf, g_recv)
+    gx_flow(start)
     g_lo = (group_grad - g_hi.astype(F32)).astype(BF16)
     byte_grad[0] = (upstream.astype(F32) + nn(picked_t, g_hi) + nn(picked_t, g_lo)).astype(BF16)
 
     @pl.when(is_att)
     def _():
-        landed(kv, kv_recv)
-        landed(qb, q_recv)
+        landed(kv.at[pl.ds(16 * r, 16)], kv_recv)
+        fw_flow(start)
+
+    landed(wq.at[0, pl.ds(0, 3), pl.ds(0, 48)], wb_recv)
+    landed(wq.at[0, pl.ds(0, 3), pl.ds(0, 48)], wc_recv)
+    wd_flow(start)
+    landed(wq.at[:, :, pl.ds(0, 48)], wd_recv)
+    landed(gq.at[pl.ds(0, 3)], gx_recv)
+
+    g_all = gq[...].reshape(256, D)
+    w_all = wq[...].reshape(D, D)
+    dop[...] = nn(g_all, w_all).astype(BF16).reshape(4, 64, D)
+    do_flow(send)
+
+    @pl.when(is_att)
+    def _():
+        landed(kv.at[pl.ds(0, 16), pl.ds(0, 144)], fw_recv)
         kt[...] = kv[:, 0:64, :].reshape(2048, HEAD_DIM).T
         vt[...] = kv[:, 64:128, :].reshape(2048, HEAD_DIM).T
         lane = lax.broadcasted_iota(jnp.int32, (1, 128), 1).astype(F32)
@@ -248,18 +309,18 @@
             kkb[:, p * 128:(p + 1) * 128] = jnp.broadcast_to(row, (8, 128))
 
         def forward(i, _):
-            queries = qb[pl.ds(2 * i, 2)].reshape(256, HEAD_DIM)
             slot = lax.broadcasted_iota(jnp.int32, (64, 128), 0).astype(F32)
-            places = []
+            places, queries = [], []
             for mm in range(2):
                 for k in range(2):
                     block = 8 * (2 * r + k) + 2 * i + mm
                     cnt = kv[block, 128:144, :].astype(F32)[0:1]
                     base = (block * 64).astype(F32)
                     places.append(jnp.where(slot < cnt, slot + base, FAR_QUERY))
+                    queries.append(kv[block, 144:208, :])
             place = jnp.concatenate(places, axis=0)
             place = jnp.concatenate([place] * 16, axis=1)
-            scores = nn(queries, kt[...])
+            scores = nn(jnp.concatenate(queries, axis=0), kt[...])
             scores = jnp.where(jnp.broadcast_to(kkb[0:1], (256, 2048)) <= place, scores, -jnp.inf)
             top = jnp.max(scores, axis=1, keepdims=True)
             attention = jnp.exp2((scores - top) * SCALE_LOG2E)
@@ -276,27 +337,14 @@
 
         lax.fori_loop(0, 4, forward, 0)
 
-    landed(wq.at[pl.ds(0, 7)], w_recv)
-    landed(gq, g_recv)
-    g_all = gq[...].reshape(256, D)
-    w_all = wq[...].reshape(D, D)
-    dop[...] = nn(g_all, w_all).astype(BF16).reshape(4, 64, D)
-    do_flow(send)
-
-    landed(ab, a_recv)
-    a_all = ab[...].reshape(256, D)
-    pp[...] = nt(a_all, w_all).astype(BF16).reshape(4, 64, D)
-    p_flow(send)
-    wgp[...] = nn(g_all.T, a_all).astype(BF16).reshape(8, 96, D)
-    wg_flow(lambda *a: remote(*a).start())
-
     @pl.when(is_att)
     def _():
         landed(dob, do_recv)
         acc[...] = jnp.zeros_like(acc)
 
         def backward(i, _):
-            queries = qb[pl.ds(2 * i, 2)].reshape(256, HEAD_DIM)
+            queries = jnp.concatenate(
+                [kv[8 * (2 * r + k) + 2 * i + mm, 144:208, :] for mm in range(2) for k in range(2)], axis=0)
             grad = dob[0, pl.ds(2 * i, 2)].astype(F32)
             for j in range(1, 4):
                 grad = grad + dob[j, pl.ds(2 * i, 2)].astype(F32)
@@ -331,11 +379,32 @@
 
         lax.fori_loop(0, 16, out, 0)
 
+    landed(ab, a_recv)
+    a_all = ab[...].reshape(256, D)
+    wgp[...] = nn(gq[...].reshape(256, D).T, a_all).reshape(2, 4, 96, D)
+    wgs[...] = wgp[:, :, pl.ds(pl.multiple_of(48 * (1 - r), 16), 48)].astype(BF16)
+    w0_flow(start)
+    pp[...] = nt(a_all, wq[...].reshape(D, D)).astype(BF16).reshape(4, 64, D)
+    px_flow(start)
+    landed(wg0, w0_recv)
+    wh[...] = (wgp[:, :, mine48] + wg0[...].astype(F32)).astype(BF16)
+    w1_flow(start)
+
+    landed(p1.at[pl.ds(0, 3)], px_recv)
+    p1[x] = pp[x]
+    ps[...] = (p1[0].astype(F32) + p1[1].astype(F32) + p1[2].astype(F32) + p1[3].astype(F32)).astype(BF16)
+    p_flow(send)
+
+    landed(wg1.at[pl.ds(0, 3)], w1_recv)
+    wg1[y] = wh[:, y]
+    total_w = wg1[0].astype(F32)
+    for i in range(1, 4):
+        total_w = total_w + wg1[i].astype(F32)
+    wt[...] = total_w.astype(BF16)
+    w2_flow(start)
+
     landed(pr, p_recv)
-    total = grows[...]
-    for i in range(4):
-        total = total + pr[i].astype(F32)
-    group_out = total.astype(BF16)
+    group_out = (grows[...] + pr[...].astype(F32)).astype(BF16)
     lrow[...] = jnp.broadcast_to(
         jnp.sum(jnp.where(last, group_out.astype(F32), 0.0), axis=0, keepdims=True), (16, D)
     ).astype(BF16)
@@ -344,13 +413,10 @@
     def _():
         row_copy.start()
 
-    landed(wgr.at[pl.ds(0, 7)], wg_recv)
-    wgr[m] = wgp[m]
-    total_w = wgr[0].astype(F32)
-    for i in range(1, 8):
-        total_w = total_w + wgr[i].astype(F32)
-    wsum[...] = total_w
-    wsum_copy.start()
+    landed(wg2, w2_recv)
+    wsum[...] = wt[zp].astype(F32) + wg2[...].astype(F32)
+    ws_flow(start)
+    wg_out[mine48] = wsum[...]
 
     @pl.when(s > 0)
     def _():
@@ -361,22 +427,17 @@
     part = jnp.sum(sel_s[...] * cross, axis=0, keepdims=True)
     cpart[...] = jnp.broadcast_to(part, (8, NB))
     call[x] = cpart[...]
-    c_flow(lambda *a: remote(*a).start())
-
-    wsum_copy.wait_recv()
-    wg_out[...] = wsum[...] + wsib[...]
+    c_flow(start)
     landed(call.at[pl.ds(0, 3)], c_recv)
     conf_grad[...] = (call[0] + call[1] + call[2] + call[3])[0:1]
 
+    landed(wsum, ws_recv)
     kv_flow(sent)
-    q_flow(sent)
-    w_flow(sent)
     g_flow(sent)
     do_flow(sent)
     p_flow(sent)
-    wg_flow(sent)
-    c_flow(sent)
-    wsum_copy.wait_send()
+    for flow in (wa_flow, wb_flow, wc_flow, wd_flow, gx_flow, px_flow, w0_flow, w1_flow, w2_flow, ws_flow, c_flow):
+        flow(finish)
 
     @pl.when(s > 0)
     def _():
@@ -388,6 +449,7 @@
 
     @pl.when(is_att)
     def _():
+        fw_flow(finish)
         ex_copy.wait_send()
 
         def one(j, _):
@@ -423,10 +485,9 @@
         in_specs=[vmem] * 8,
         out_specs=(vmem,) * 6,
         scratch_shapes=[
-            pltpu.VMEM((NH, 144, 128), BF16),
-            pltpu.VMEM((NS, 144, 128), BF16),
-            pltpu.VMEM((8, 2, 64, 128), BF16),
-            pltpu.VMEM((8, 96, D), BF16),
+            pltpu.VMEM((NH, 208, 128), BF16),
+            pltpu.VMEM((NS, 208, 128), BF16),
+            pltpu.VMEM((2, 4, 96, D), BF16),
             pltpu.VMEM((80, D), F32),
             pltpu.VMEM((8, D), F32),
             pltpu.VMEM((64, D), BF16),
@@ -442,10 +503,16 @@
             pltpu.VMEM((4, 64, D), BF16),
             pltpu.VMEM((4, 64, D), BF16),
             pltpu.VMEM((4, 64, D), BF16),
-            pltpu.VMEM((8, 96, D), BF16),
-            pltpu.VMEM((8, 96, D), BF16),
-            pltpu.VMEM((96, D), F32),
-            pltpu.VMEM((96, D), F32),
+            pltpu.VMEM((64, D), BF16),
+            pltpu.VMEM((64, D), BF16),
+            pltpu.VMEM((2, 4, 96, D), F32),
+            pltpu.VMEM((2, 4, 48, D), BF16),
+            pltpu.VMEM((2, 4, 48, D), BF16),
+            pltpu.VMEM((2, 4, 48, D), BF16),
+            pltpu.VMEM((4, 2, 48, D), BF16),
+            pltpu.VMEM((2, 48, D), BF16),
+            pltpu.VMEM((48, D), BF16),
+            pltpu.VMEM((48, D), F32),
             pltpu.VMEM((16, D), BF16),
             pltpu.VMEM((16, D), BF16),
             pltpu.VMEM((8, NB), F32),
@@ -456,15 +523,22 @@
             pltpu.VMEM((2, 16, 64, 128), BF16),
             pltpu.VMEM((80, NB), F32),
             pltpu.VMEM((64, D), F32),
-            dma((12,)), dma,
             dma((6,)), dma,
-            dma((7,)), dma,
-            dma, dma,
-            dma((4,)), dma,
+            dma, dma,
+            dma, dma,
+            dma((3,)), dma,
+            dma((3,)), dma,
+            dma, dma,
+            dma, dma,
+            dma, dma,
+            dma((3,)), dma,
             dma((12,)), dma,
             dma((32,)), dma,
-            dma((4,)), dma,
-            dma((7,)), dma,
+            dma((3,)), dma,
+            dma, dma,
+            dma, dma,
+            dma((3,)), dma,
+            dma, dma,
             dma, dma,
             dma, dma,
             dma((3,)), dma,

time: 130 us -> 97.6 us (0.75)
  the two profiles are of different devices: /device:TPU:24 before, /device:TPU:68 now
where the time goes in v2:
time: 97.6 us; the launch traced here: 96 us
  Pallas kernels  90.3 us (93%)
  local copies, waits for them, and re-layouts  5.03 us (5%)
    pallas_call x1, Pallas kernels, local(): pl.pallas_call(kernel, out_shape=(jax.ShapeDtypeStruct((1, NB, D), BF16),...  90.3 us
    unnamed x16, local copies, waits for them, and re-layouts  5.03 us

profile of v2, /device:TPU:68, one launch (start us, length us, event | category | flops | bytes accessed | tf_op | source)
XLA Modules:
  0.0 96.0 jit_solution(17005594256355721864)
XLA Ops:
  0.6 90.3 %shard_map.127 = (bf16[1,256,768]{2,1,0:T(8,128)(2,1)}, f32[1,256]{1,0:T(1,128)}, bf16[1,64,768]{2,1,0:T(8,128)(2,1)}, bf16[1,64,768]{2,1,0:T(8,128)(2,1)}, bf16...) custom-call(bf16[1,256,768]{2,1,0:T(8,128)(2,1)} %states.1, s32[1,256]{1,0:T(1,128)} %starts.1, f32[1,256]{1,0:T(1,128)} %conf.1, ...), custom_call_target="tpu_custom_call" | custom-call | flops 8000000000 | bytes 20000000 | tf_op jit(solution)/shard_map/pallas_call | solution.py:477
  91.0 0.0 copy-start.4
  91.0 0.0 copy-start.3
  91.0 0.0 copy-start.2
  91.0 0.0 copy-start.1
  91.0 1.8 %copy.20 = bf16[1,256,768]{2,1,0:T(8,128)(2,1)} copy(bf16[1,256,768]{2,1,0:T(8,128)(2,1)} %get-tuple-element.12) | data formatting | bytes 786432
  92.8 0.0 copy-done.4
  92.8 0.6 copy.21
  93.4 0.0 copy-done.3
  93.4 0.0 copy-start
  93.4 0.6 copy.22
  94.0 0.0 copy-done.2
  94.0 0.6 copy.23
  94.7 0.0 copy-done.1
  94.7 0.6 copy.24
  95.3 0.0 copy-done
  95.3 0.7 copy.25
Async XLA Ops:
  91.0 1.9 %copy-start.4 = (f32[1,256]{1,0:T(1,128)S(1)}, f32[1,256]{1,0:T(1,128)}, u32[]{:S(2)}) copy-start(f32[1,256]{1,0:T(1,128)} %get-tuple-element.13) | copy-start | bytes 3076
  91.0 2.4 %copy-start.3 = (bf16[1,64,768]{2,1,0:T(8,128)(2,1)S(1)}, bf16[1,64,768]{2,1,0:T(8,128)(2,1)}, u32[]{:S(2)}) copy-start(bf16[1,64,768]{2,1,0:T(8,128)(2,1)} %get-tuple-element.14) | copy-start | bytes 294916
  91.0 3.0 %copy-start.2 = (bf16[1,64,768]{2,1,0:T(8,128)(2,1)S(1)}, bf16[1,64,768]{2,1,0:T(8,128)(2,1)}, u32[]{:S(2)}) copy-start(bf16[1,64,768]{2,1,0:T(8,128)(2,1)} %get-tuple-element.15) | copy-start | bytes 294916
  91.0 3.7 %copy-start.1 = (bf16[1,64,768]{2,1,0:T(8,128)(2,1)S(1)}, bf16[1,64,768]{2,1,0:T(8,128)(2,1)}, u32[]{:S(2)}) copy-start(bf16[1,64,768]{2,1,0:T(8,128)(2,1)} %get-tuple-element.16) | copy-start | bytes 294916
  93.4 1.9 %copy-start = (f32[96,768]{1,0:T(8,128)S(1)}, f32[96,768]{1,0:T(8,128)}, u32[]{:S(2)}) copy-start(f32[96,768]{1,0:T(8,128)} %get-tuple-element.17) | copy-start | bytes 884740

commit v3 on v2

--- a/solution.py
+++ b/solution.py
@@ -260,7 +260,6 @@
         spill_copy.start()
 
     wa_flow(start)
-    kv_flow(send)
     wb_flow(start)
 
     @pl.when(s < NS - 1)
@@ -272,6 +271,7 @@
     g_hi = group_grad.astype(BF16)
     g_bf[...] = g_hi
     g_flow(send)
+    kv_flow(send)
     landed(w_in.at[pl.ds(0, 48)], wa_recv)
     wc_flow(start)
     landed(g_bf, g_recv)
@@ -279,11 +279,6 @@
     g_lo = (group_grad - g_hi.astype(F32)).astype(BF16)
     byte_grad[0] = (upstream.astype(F32) + nn(picked_t, g_hi) + nn(picked_t, g_lo)).astype(BF16)
 
-    @pl.when(is_att)
-    def _():
-        landed(kv.at[pl.ds(16 * r, 16)], kv_recv)
-        fw_flow(start)
-
     landed(wq.at[0, pl.ds(0, 3), pl.ds(0, 48)], wb_recv)
     landed(wq.at[0, pl.ds(0, 3), pl.ds(0, 48)], wc_recv)
     wd_flow(start)
@@ -297,6 +292,8 @@
 
     @pl.when(is_att)
     def _():
+        landed(kv.at[pl.ds(16 * r, 16)], kv_recv)
+        fw_flow(start)
         landed(kv.at[pl.ds(0, 16), pl.ds(0, 144)], fw_recv)
         kt[...] = kv[:, 0:64, :].reshape(2048, HEAD_DIM).T
         vt[...] = kv[:, 64:128, :].reshape(2048, HEAD_DIM).T
@@ -369,16 +366,6 @@
 
         lax.fori_loop(0, 4, backward, 0)
         ex_copy.start()
-        ex_copy.wait_recv()
-        dkf[0] = ((acc[r, 0] + sib[0]) * SCALE).T.astype(BF16).reshape(16, 64, HEAD_DIM)
-        dkf[1] = (acc[r, 1] + sib[1]).T.astype(BF16).reshape(16, 64, HEAD_DIM)
-
-        def out(j, _):
-            dkv_flow(send, j)
-            return 0
-
-        lax.fori_loop(0, 16, out, 0)
-
     landed(ab, a_recv)
     a_all = ab[...].reshape(256, D)
     wgp[...] = nn(gq[...].reshape(256, D).T, a_all).reshape(2, 4, 96, D)
@@ -386,6 +373,19 @@
     w0_flow(start)
     pp[...] = nt(a_all, wq[...].reshape(D, D)).astype(BF16).reshape(4, 64, D)
     px_flow(start)
+
+    @pl.when(is_att)
+    def _():
+        ex_copy.wait_recv()
+        dkf[0] = ((acc[r, 0] + sib[0]) * SCALE).T.astype(BF16).reshape(16, 64, HEAD_DIM)
+        dkf[1] = (acc[r, 1] + sib[1]).T.astype(BF16).reshape(16, 64, HEAD_DIM)
+
+        def out(j, _):
+            dkv_flow(send, j)
+            return 0
+
+        lax.fori_loop(0, 16, out, 0)
+
     landed(wg0, w0_recv)
     wh[...] = (wgp[:, :, mine48] + wg0[...].astype(F32)).astype(BF16)
     w1_flow(start)
@@ -470,18 +470,32 @@
     landed(dv_out, dv_recv)
 
 
+def hand_over(*refs):
+    held, sems = refs[12:18], refs[18]
+    come = [pltpu.make_async_copy(refs[i], held[i], sems.at[i]) for i in range(6)]
+    leave = [pltpu.make_async_copy(held[i], refs[6 + i], sems.at[6 + i]) for i in range(6)]
+    for copy in come:
+        copy.start()
+    for i in range(6):
+        come[i].wait()
+        leave[i].start()
+    for copy in leave:
+        copy.wait()
+
+
 def local(byte_states, boundary, confidence, query_rows, key_rows, value_rows, out_weight, upstream):
     vmem = pl.BlockSpec(memory_space=pltpu.VMEM)
     dma = pltpu.SemaphoreType.DMA
     rows = jax.ShapeDtypeStruct((1, CAP, D), BF16)
-    return pl.pallas_call(
+    shapes = (
+        jax.ShapeDtypeStruct((1, NB, D), BF16),
+        jax.ShapeDtypeStruct((1, NB), F32),
+        rows, rows, rows,
+        jax.ShapeDtypeStruct((96, D), F32),
+    )
+    parts = pl.pallas_call(
         kernel,
-        out_shape=(
-            jax.ShapeDtypeStruct((1, NB, D), BF16),
-            jax.ShapeDtypeStruct((1, NB), F32),
-            rows, rows, rows,
-            jax.ShapeDtypeStruct((96, D), F32),
-        ),
+        out_shape=shapes,
         in_specs=[vmem] * 8,
         out_specs=(vmem,) * 6,
         scratch_shapes=[
@@ -552,6 +566,15 @@
         ),
         cost_estimate=pl.CostEstimate(flops=8_000_000_000, bytes_accessed=20_000_000, transcendentals=3_000_000),
     )(byte_states, boundary, confidence, query_rows, key_rows, value_rows, out_weight, upstream)
+    whole = pl.BlockSpec(memory_space=pl.ANY)
+    return pl.pallas_call(
+        hand_over,
+        out_shape=shapes,
+        in_specs=[whole] * 6,
+        out_specs=(whole,) * 6,
+        scratch_shapes=[pltpu.VMEM(shape.shape, shape.dtype) for shape in shapes] + [dma((12,))],
+        compiler_params=pltpu.CompilerParams(vmem_limit_bytes=60 * 1024 * 1024),
+    )(*parts)
 
 
 def solution(mesh):

time: 97.6 us -> 89.6 us (0.918)
  the two profiles are of different devices: /device:TPU:68 before, /device:TPU:24 now
where the time goes in v3:
time: 89.6 us; the launch traced here: 89.5 us
  Pallas kernels  88.8 us (99%)
    pallas_call x1, Pallas kernels, local(): pl.pallas_call(kernel, out_shape=shapes, in_specs=[vmem] * 8, out_specs=(...  86.8 us
    pallas_call x1, Pallas kernels, local(): pl.pallas_call(hand_over, out_shape=shapes, in_specs=[whole] * 6, out_spe...  2.05 us

profile of v3, /device:TPU:24, one launch (start us, length us, event | category | flops | bytes accessed | tf_op | source)
XLA Modules:
  0.0 89.5 jit_solution(10305992376695966670)
XLA Ops:
  0.6 86.8 %shard_map.127 = (bf16[1,256,768]{2,1,0:T(8,128)(2,1)}, f32[1,256]{1,0:T(1,128)}, bf16[1,64,768]{2,1,0:T(8,128)(2,1)}, bf16[1,64,768]{2,1,0:T(8,128)(2,1)}, bf16...) custom-call(bf16[1,256,768]{2,1,0:T(8,128)(2,1)} %states.1, s32[1,256]{1,0:T(1,128)} %starts.1, f32[1,256]{1,0:T(1,128)} %conf.1, ...), custom_call_target="tpu_custom_call" | custom-call | flops 8000000000 | bytes 20000000 | tf_op jit(solution)/shard_map/pallas_call | solution.py:496
  87.4 2.0 %shard_map.128 = (bf16[1,256,768]{2,1,0:T(8,128)(2,1)}, f32[1,256]{1,0:T(1,128)}, bf16[1,64,768]{2,1,0:T(8,128)(2,1)}, bf16[1,64,768]{2,1,0:T(8,128)(2,1)}, bf16...) custom-call(bf16[1,256,768]{2,1,0:T(8,128)(2,1)} %get-tuple-element.12.refs_0_, f32[1,256]{1,0:T(1,128)} %get-tuple-element.13.refs_1_, ...), custom_call_target="tpu_custom_call" | custom-call | tf_op jit(solution)/shard_map/pallas_call | solution.py:570

commit v4 on v3

--- a/solution.py
+++ b/solution.py
@@ -35,13 +35,13 @@
 def kernel(
     states, starts, conf, q_in, k_in, v_in, w_in, up,
     byte_grad, conf_grad, dq_out, dk_out, dv_out, wg_out,
-    stage, kv, wq, gext, spill_in, g_bf, gq, dop, dob,
-    kt, vt, kkb, probs, inv, a_out, ab, pp, p1, ps, pr, wgp, wgs, wg0, wh, wg1, wt, wg2, wsum,
+    stage, kv, wq, gext, spill_in, perm, pack, gp, gr, gq, dop, dr, og, dob,
+    kt, vt, kkb, probs, inv, a_out, ab, pp, p1, ps4, pr, wgp, wgs, wg0, wh, wg1, rl, rs, wsum,
     lrow, prow, cpart, call, dqb, acc, sib, dkf, sel_s, grows,
-    kv_send, kv_recv, fw_send, fw_recv, wa_send, wa_recv, wb_send, wb_recv, wc_send, wc_recv, wd_send, wd_recv,
-    sp_send, sp_recv, g_send, g_recv, gx_send, gx_recv,
-    do_send, do_recv, a_send, a_recv, px_send, px_recv, p_send, p_recv,
-    w0_send, w0_recv, w1_send, w1_recv, w2_send, w2_recv, ws_send, ws_recv,
+    kv_send, kv_recv, fw_send, fw_recv, wa_send, wa_recv, wb_send, wb_recv, wd_send, wd_recv,
+    sp_send, sp_recv, g_send, g_recv, gx_send, gx_recv, dr_send, dr_recv,
+    do_send, do_recv, a_send, a_recv, ay_send, ay_recv, px_send, px_recv, p_send, p_recv,
+    w0_send, w0_recv, w1_send, w1_recv, rl_send, rl_recv, ws_send, ws_recv,
     lr_send, lr_recv, c_send, c_recv, dq_send, dq_recv, dk_send, dk_recv, dv_send, dv_recv,
     ex_send, ex_recv,
 ):
@@ -50,7 +50,7 @@
     r = lax.axis_index("rep")
     q = lax.div(s, 8)
     m = lax.rem(s, 8)
-    zp = lax.div(m, 4)
+    z = lax.div(s, 4)
     y = lax.rem(m, 4)
     half = lax.div(q, 2)
     att = lax.div(3 * s + 7, 8)
@@ -93,69 +93,85 @@
         return pl.ds(h * HEAD_DIM if isinstance(h, int) else pl.multiple_of(h * HEAD_DIM, HEAD_DIM), HEAD_DIM)
 
     mine48 = pl.ds(pl.multiple_of(48 * r, 16), 48)
-    z_peer = (s + 4 - 8 * zp, x, r)
     sib_id = (s, x, 1 - r)
 
     def y_peer(i):
         return (s - y + lax.rem(y + i, 4), x, r)
 
+    def z_place(i):
+        return lax.rem(z + i, 8)
+
+    def z_peer(i):
+        return (4 * z_place(i) + y, x, r)
+
     def x_peer(i):
         return (s, lax.rem(x + i, 4), r)
 
     def kv_flow(op):
-        for h in range(NH):
-            op(stage.at[h], kv.at[s], kv_send.at[h], kv_recv, (att_seq(h, r), x, half))
+        for i in range(NH):
+            h = lax.rem(s + 3 * r + i, NH)
+            op(stage.at[h], kv.at[s], kv_send.at[i], kv_recv, (att_seq(h, r), x, half))
+
+    even = lax.rem(z, 2) == 0
 
     def wa_flow(op):
-        op(w_in.at[mine48], wq.at[zp, y, mine48], wa_send, wa_recv, z_peer)
+        for j, i in enumerate((1, 7, 2, 6)):
+            op(w_in.at[mine48], wq.at[z, mine48], wa_send.at[j], wa_recv.at[j], z_peer(i))
 
     def wb_flow(op):
-        for i in range(1, 4):
-            op(w_in.at[mine48], wq.at[zp, y, mine48], wb_send.at[i - 1], wb_recv, y_peer(i))
-
-    def wc_flow(op):
-        for i in range(1, 4):
-            op(wq.at[1 - zp, y, mine48], wq.at[1 - zp, y, mine48], wc_send.at[i - 1], wc_recv, y_peer(i))
+        for j, (block, i) in enumerate(((6, 1), (2, 7), (jnp.where(even, 6, 2), jnp.where(even, 2, 6)))):
+            part = wq.at[z_place(block), mine48]
+            op(part, part, wb_send.at[j], wb_recv, z_peer(i))
 
     def wd_flow(op):
-        op(wq.at[:, :, mine48], wq.at[:, :, mine48], wd_send, wd_recv, sib_id)
-
-    turned = (8 * x + m, q, r)
+        op(wq.at[:, mine48], wq.at[:, mine48], wd_send, wd_recv, sib_id)
 
     def g_flow(op):
-        op(g_bf, gq.at[q], g_send, g_recv, turned)
+        for i in range(4):
+            op(gp.at[i], gr.at[x], g_send.at[i], g_recv, (4 * z + i, y, r))
 
     def gx_flow(op):
         for i in range(1, 4):
             op(gq.at[x], gq.at[x], gx_send.at[i - 1], gx_recv, x_peer(i))
 
+    def dr_flow(op):
+        for i in range(1, 4):
+            op(dop.at[lax.rem(y + i, 4)], dr.at[y], dr_send.at[i - 1], dr_recv, y_peer(i))
+
     def do_flow(op):
-        for h in range(NH):
-            for c in range(2):
-                op(dop.at[pl.ds(2 * c, 2), :, lanes(h)], dob.at[q, m], do_send.at[2 * h + c], do_recv,
-                   (att_seq(h, r), x, c))
+        for i in range(NH):
+            h = lax.rem(s + 3 * r + i, NH)
+            op(og.at[:, lanes(h)], dob.at[m, lax.rem(q, 2)], do_send.at[i], do_recv, (att_seq(h, r), x, half))
 
     def a_flow(op, mm):
-        for i in range(4):
-            op(a_out.at[mm], ab.at[pl.ds(2 * r, 2), :, lanes(att_h)], a_send.at[mm * 4 + i], a_recv,
-               (8 * i + mm, x, att_w))
+        for k in range(2):
+            op(a_out.at[mm, k], ab.at[lax.rem(mm, 4), :, lanes(att_h)], a_send.at[mm * 2 + k], a_recv,
+               (8 * (2 * r + k) + mm, x, att_w))
+
+    def ay_flow(op):
+        for i in range(1, 4):
+            op(ab.at[y], ab.at[y], ay_send.at[i - 1], ay_recv, y_peer(i))
 
     def px_flow(op):
         for i in range(1, 4):
             op(pp.at[lax.rem(x + i, 4)], p1.at[x], px_send.at[i - 1], px_recv, x_peer(i))
 
     def p_flow(op):
-        op(ps, pr, p_send, p_recv, turned)
+        for i in range(4):
+            op(ps4.at[i], pr.at[y], p_send.at[i], p_recv, (4 * z + x, i, r))
 
     def w0_flow(op):
         op(wgs, wg0, w0_send, w0_recv, sib_id)
 
     def w1_flow(op):
-        for i in range(1, 4):
-            op(wh.at[:, lax.rem(y + i, 4)], wg1.at[y], w1_send.at[i - 1], w1_recv, y_peer(i))
+        for j, i in enumerate((1, 7)):
+            op(wh.at[z_place(i)], wg1.at[j], w1_send.at[j], w1_recv.at[j], z_peer(i))
+        for j, (block, i) in enumerate(((3, 1), (5, 7), (4, jnp.where(even, 2, 6)))):
+            op(wh.at[z_place(block)], rl.at[j], rl_send.at[j], rl_recv.at[j], z_peer(i))
 
     def w2_flow(op):
-        op(wt.at[1 - zp], wg2, w2_send, w2_recv, z_peer)
+        for j, i in enumerate((2, 6)):
+            op(rs.at[j], wg1.at[2 + j], w1_send.at[2 + j], w1_recv.at[2 + j], z_peer(i))
 
     def ws_flow(op):
         op(wsum, wg_out.at[mine48], ws_send, ws_recv, sib_id)
@@ -194,8 +210,11 @@
     for i in range(1, 4):
         greet(y_peer(i))
         greet(x_peer(i))
-    greet(z_peer)
-    greet(turned)
+    for i in (1, 2, 6, 7):
+        greet(z_peer(i))
+    for i in range(4):
+        greet((4 * z + i, y, r))
+        greet((4 * z + x, i, r))
     greet(sib_id)
 
     @pl.when(s > 0)
@@ -237,7 +256,14 @@
     picked = sel[0:64] * start_row
     picked_t = picked.T.astype(BF16)
     grows[...] = nn(picked.astype(BF16), states[0])
-    wq[zp, y, mine48] = w_in[mine48]
+    wq[z, mine48] = w_in[mine48]
+    last = lax.broadcasted_iota(jnp.int32, (64, D), 0).astype(F32) == count - 1.0
+    place = lax.broadcasted_iota(jnp.int32, (1, 1024), 1)
+    group, at = lax.div(place, 256), lax.rem(place, 256)
+    source = jnp.where(at < 96, 96 * group + at, jnp.where(at < 192, 96 * group + 288 + at, -1))
+    perm[...] = jnp.where(lax.broadcasted_iota(jnp.int32, (D, 1024), 0) == source, 1.0, 0.0).astype(BF16)
+    packed = jnp.where(at < 192, 192 * group + at, -1)
+    pack[...] = jnp.where(lax.broadcasted_iota(jnp.int32, (D, 1024), 0) == packed, 1.0, 0.0).astype(BF16)
 
     @pl.when(s == NS - 1)
     def _():
@@ -248,8 +274,8 @@
         prow[...] = jnp.zeros_like(prow)
 
     partners = (
-        12 + 3 + 3 + 1 + 1
-        + jnp.where(q == x, 0, 1)
+        12 + 3 + 3 + 4 + 8 + 1
+        - jnp.where(x == y, 2, 0)
         + jnp.where(s > 0, 1, 0) + jnp.where(s < NS - 1, 1, 0)
         + jnp.where(is_att, jnp.where(att_w == r, 30, 32), 0)
     )
@@ -259,36 +285,29 @@
     def _():
         spill_copy.start()
 
+    kv_flow(send)
     wa_flow(start)
-    wb_flow(start)
 
     @pl.when(s < NS - 1)
     def _():
         spill_copy.wait_recv()
 
-    last = lax.broadcasted_iota(jnp.int32, (64, D), 0).astype(F32) == count - 1.0
     group_grad = gext[0:64] + jnp.where(last, spill_in[0:1], 0.0)
     g_hi = group_grad.astype(BF16)
-    g_bf[...] = g_hi
+    spread = nn(g_hi, perm[...]).astype(BF16)
+    for i in range(4):
+        gp[i] = spread[:, 256 * i:256 * (i + 1)]
     g_flow(send)
-    kv_flow(send)
-    landed(w_in.at[pl.ds(0, 48)], wa_recv)
-    wc_flow(start)
-    landed(g_bf, g_recv)
-    gx_flow(start)
     g_lo = (group_grad - g_hi.astype(F32)).astype(BF16)
     byte_grad[0] = (upstream.astype(F32) + nn(picked_t, g_hi) + nn(picked_t, g_lo)).astype(BF16)
 
-    landed(wq.at[0, pl.ds(0, 3), pl.ds(0, 48)], wb_recv)
-    landed(wq.at[0, pl.ds(0, 3), pl.ds(0, 48)], wc_recv)
-    wd_flow(start)
-    landed(wq.at[:, :, pl.ds(0, 48)], wd_recv)
-    landed(gq.at[pl.ds(0, 3)], gx_recv)
-
-    g_all = gq[...].reshape(256, D)
-    w_all = wq[...].reshape(D, D)
-    dop[...] = nn(g_all, w_all).astype(BF16).reshape(4, 64, D)
-    do_flow(send)
+    landed(gr, g_recv)
+    gathered = jnp.concatenate([gr[0], gr[1], gr[2], gr[3]], axis=1)
+    gq[x] = nt(gathered, pack[...]).astype(BF16)
+    gx_flow(start)
+    for j in (2, 3):
+        landed(w_in.at[pl.ds(0, 48)], wa_recv.at[j])
+    wb_flow(start)
 
     @pl.when(is_att)
     def _():
@@ -305,7 +324,8 @@
             row = jnp.where(live > 0.0, lane + 128.0 * p, FAR_KEY)
             kkb[:, p * 128:(p + 1) * 128] = jnp.broadcast_to(row, (8, 128))
 
-        def forward(i, _):
+        def forward(step, _):
+            i = lax.rem(step + att, 4)
             slot = lax.broadcasted_iota(jnp.int32, (64, 128), 0).astype(F32)
             places, queries = [], []
             for mm in range(2):
@@ -334,18 +354,63 @@
 
         lax.fori_loop(0, 4, forward, 0)
 
+    for j in (0, 1):
+        landed(w_in.at[pl.ds(0, 48)], wa_recv.at[j])
+    landed(wq.at[pl.ds(0, 3), pl.ds(0, 48)], wb_recv)
+    wd_flow(start)
+    landed(gq.at[pl.ds(0, 3)], gx_recv)
+    landed(wq.at[:, pl.ds(0, 48)], wd_recv)
+
+    g_all = gq[...].reshape(256, D)
+    w_all = wq[...].reshape(D, D)
+    dop[...] = nn(g_all, w_all).astype(BF16).reshape(4, 64, D)
+    dr_flow(start)
+    landed(w_in.at[pl.ds(0, 64)], a_recv)
+    ay_flow(start)
+
+    landed(dr.at[pl.ds(0, 3)], dr_recv)
+    dr[y] = dop[y]
+    og[...] = (dr[0].astype(F32) + dr[1].astype(F32) + dr[2].astype(F32) + dr[3].astype(F32)).astype(BF16)
+    do_flow(send)
+
+    landed(ab.at[pl.ds(0, 3)], ay_recv)
+    a_all = ab[...].reshape(256, D)
+    pp[...] = nt(a_all, wq[...].reshape(D, D)).astype(BF16).reshape(4, 64, D)
+    px_flow(start)
+    wgp[...] = nn(gq[...].reshape(256, D).T, a_all).reshape(8, 96, D)
+    wgs[...] = wgp[:, pl.ds(pl.multiple_of(48 * (1 - r), 16), 48)].astype(BF16)
+    w0_flow(start)
+
+
+    landed(wg0, w0_recv)
+    wh[...] = (wgp[:, mine48] + wg0[...].astype(F32)).astype(BF16)
+    w1_flow(start)
+
+    landed(p1.at[pl.ds(0, 3)], px_recv)
+    p1[x] = pp[x]
+    summed = (p1[0].astype(F32) + p1[1].astype(F32) + p1[2].astype(F32) + p1[3].astype(F32)).astype(BF16)
+    apart = nn(summed, pack[...]).astype(BF16)
+    for i in range(4):
+        ps4[i] = apart[:, 256 * i:256 * (i + 1)]
+    p_flow(send)
+
+    for j in range(3):
+        landed(rl.at[j], rl_recv.at[j])
+    far = rl[2].astype(F32)
+    rs[0] = (wh[z_place(2)].astype(F32) + rl[0].astype(F32) + jnp.where(even, far, 0.0)).astype(BF16)
+    rs[1] = (wh[z_place(6)].astype(F32) + rl[1].astype(F32) + jnp.where(even, 0.0, far)).astype(BF16)
+    w2_flow(start)
+
     @pl.when(is_att)
     def _():
         landed(dob, do_recv)
         acc[...] = jnp.zeros_like(acc)
 
-        def backward(i, _):
+        def backward(step, _):
+            i = lax.rem(step + att, 4)
             queries = jnp.concatenate(
                 [kv[8 * (2 * r + k) + 2 * i + mm, 144:208, :] for mm in range(2) for k in range(2)], axis=0)
-            grad = dob[0, pl.ds(2 * i, 2)].astype(F32)
-            for j in range(1, 4):
-                grad = grad + dob[j, pl.ds(2 * i, 2)].astype(F32)
-            grad = grad.reshape(256, HEAD_DIM).astype(BF16).astype(F32)
+            grad = dob[pl.ds(2 * i, 2)].reshape(256, HEAD_DIM).astype(F32)
             grad = (grad * inv[i]).astype(BF16)
             attended = a_out[pl.ds(2 * i, 2)].reshape(256, HEAD_DIM)
             dots = jnp.sum(grad.astype(F32) * attended.astype(F32), axis=1, keepdims=True)
@@ -366,45 +431,18 @@
 
         lax.fori_loop(0, 4, backward, 0)
         ex_copy.start()
-    landed(ab, a_recv)
-    a_all = ab[...].reshape(256, D)
-    wgp[...] = nn(gq[...].reshape(256, D).T, a_all).reshape(2, 4, 96, D)
-    wgs[...] = wgp[:, :, pl.ds(pl.multiple_of(48 * (1 - r), 16), 48)].astype(BF16)
-    w0_flow(start)
-    pp[...] = nt(a_all, wq[...].reshape(D, D)).astype(BF16).reshape(4, 64, D)
-    px_flow(start)
-
-    @pl.when(is_att)
-    def _():
         ex_copy.wait_recv()
         dkf[0] = ((acc[r, 0] + sib[0]) * SCALE).T.astype(BF16).reshape(16, 64, HEAD_DIM)
         dkf[1] = (acc[r, 1] + sib[1]).T.astype(BF16).reshape(16, 64, HEAD_DIM)
 
-        def out(j, _):
-            dkv_flow(send, j)
+        def out(step, _):
+            dkv_flow(send, lax.rem(step + 3 * att, 16))
             return 0
 
         lax.fori_loop(0, 16, out, 0)
-
-    landed(wg0, w0_recv)
-    wh[...] = (wgp[:, :, mine48] + wg0[...].astype(F32)).astype(BF16)
-    w1_flow(start)
-
-    landed(p1.at[pl.ds(0, 3)], px_recv)
-    p1[x] = pp[x]
-    ps[...] = (p1[0].astype(F32) + p1[1].astype(F32) + p1[2].astype(F32) + p1[3].astype(F32)).astype(BF16)
-    p_flow(send)
-
-    landed(wg1.at[pl.ds(0, 3)], w1_recv)
-    wg1[y] = wh[:, y]
-    total_w = wg1[0].astype(F32)
-    for i in range(1, 4):
-        total_w = total_w + wg1[i].astype(F32)
-    wt[...] = total_w.astype(BF16)
-    w2_flow(start)
-
     landed(pr, p_recv)
-    group_out = (grows[...] + pr[...].astype(F32)).astype(BF16)
+    gathered = jnp.concatenate([pr[0], pr[1], pr[2], pr[3]], axis=1)
+    group_out = (grows[...] + nt(gathered, perm[...])).astype(BF16)
     lrow[...] = jnp.broadcast_to(
         jnp.sum(jnp.where(last, group_out.astype(F32), 0.0), axis=0, keepdims=True), (16, D)
     ).astype(BF16)
@@ -412,11 +450,6 @@
     @pl.when(s < NS - 1)
     def _():
         row_copy.start()
-
-    landed(wg2, w2_recv)
-    wsum[...] = wt[zp].astype(F32) + wg2[...].astype(F32)
-    ws_flow(start)
-    wg_out[mine48] = wsum[...]
 
     @pl.when(s > 0)
     def _():
@@ -428,6 +461,14 @@
     cpart[...] = jnp.broadcast_to(part, (8, NB))
     call[x] = cpart[...]
     c_flow(start)
+    total_w = wh[z].astype(F32)
+    for j in range(4):
+        landed(wg1.at[j], w1_recv.at[j])
+        total_w = total_w + wg1[j].astype(F32)
+    wsum[...] = total_w
+    ws_flow(start)
+    wg_out[mine48] = wsum[...]
+
     landed(call.at[pl.ds(0, 3)], c_recv)
     conf_grad[...] = (call[0] + call[1] + call[2] + call[3])[0:1]
 
@@ -436,7 +477,7 @@
     g_flow(sent)
     do_flow(sent)
     p_flow(sent)
-    for flow in (wa_flow, wb_flow, wc_flow, wd_flow, gx_flow, px_flow, w0_flow, w1_flow, w2_flow, ws_flow, c_flow):
+    for flow in (wa_flow, wb_flow, wd_flow, gx_flow, dr_flow, ay_flow, px_flow, w0_flow, w1_flow, w2_flow, ws_flow, c_flow):
         flow(finish)
 
     @pl.when(s > 0)
@@ -501,13 +542,18 @@
         scratch_shapes=[
             pltpu.VMEM((NH, 208, 128), BF16),
             pltpu.VMEM((NS, 208, 128), BF16),
-            pltpu.VMEM((2, 4, 96, D), BF16),
+            pltpu.VMEM((8, 96, D), BF16),
             pltpu.VMEM((80, D), F32),
             pltpu.VMEM((8, D), F32),
-            pltpu.VMEM((64, D), BF16),
+            pltpu.VMEM((D, 1024), BF16),
+            pltpu.VMEM((D, 1024), BF16),
+            pltpu.VMEM((4, 64, 256), BF16),
+            pltpu.VMEM((4, 64, 256), BF16),
             pltpu.VMEM((4, 64, D), BF16),
             pltpu.VMEM((4, 64, D), BF16),
-            pltpu.VMEM((4, 8, 2, 64, 128), BF16),
+            pltpu.VMEM((4, 64, D), BF16),
+            pltpu.VMEM((64, D), BF16),
+            pltpu.VMEM((8, 2, 64, 128), BF16),
             pltpu.VMEM((128, 2048), BF16),
             pltpu.VMEM((128, 2048), BF16),
             pltpu.VMEM((8, 2048), F32),
@@ -517,15 +563,15 @@
             pltpu.VMEM((4, 64, D), BF16),
             pltpu.VMEM((4, 64, D), BF16),
             pltpu.VMEM((4, 64, D), BF16),
-            pltpu.VMEM((64, D), BF16),
-            pltpu.VMEM((64, D), BF16),
-            pltpu.VMEM((2, 4, 96, D), F32),
-            pltpu.VMEM((2, 4, 48, D), BF16),
-            pltpu.VMEM((2, 4, 48, D), BF16),
-            pltpu.VMEM((2, 4, 48, D), BF16),
-            pltpu.VMEM((4, 2, 48, D), BF16),
+            pltpu.VMEM((4, 64, 256), BF16),
+            pltpu.VMEM((4, 64, 256), BF16),
+            pltpu.VMEM((8, 96, D), F32),
+            pltpu.VMEM((8, 48, D), BF16),
+            pltpu.VMEM((8, 48, D), BF16),
+            pltpu.VMEM((8, 48, D), BF16),
+            pltpu.VMEM((4, 48, D), BF16),
+            pltpu.VMEM((3, 48, D), BF16),
             pltpu.VMEM((2, 48, D), BF16),
-            pltpu.VMEM((48, D), BF16),
             pltpu.VMEM((48, D), F32),
             pltpu.VMEM((16, D), BF16),
             pltpu.VMEM((16, D), BF16),
@@ -539,20 +585,21 @@
             pltpu.VMEM((64, D), F32),
             dma((6,)), dma,
             dma, dma,
-            dma, dma,
-            dma((3,)), dma,
+            dma((4,)), dma((4,)),
             dma((3,)), dma,
             dma, dma,
             dma, dma,
+            dma((4,)), dma,
+            dma((3,)), dma,
+            dma((3,)), dma,
+            dma((6,)), dma,
+            dma((16,)), dma,
+            dma((3,)), dma,
+            dma((3,)), dma,
+            dma((4,)), dma,
             dma, dma,
-            dma((3,)), dma,
-            dma((12,)), dma,
-            dma((32,)), dma,
-            dma((3,)), dma,
-            dma, dma,
-            dma, dma,
-            dma((3,)), dma,
-            dma, dma,
+            dma((4,)), dma((4,)),
+            dma((3,)), dma((3,)),
             dma, dma,
             dma, dma,
             dma((3,)), dma,

time: 89.6 us -> 82.9 us (0.925)
  the two profiles are of different devices: /device:TPU:24 before, /device:TPU:64 now
where the time goes in v4:
time: 82.9 us; the launch traced here: 82.7 us
  Pallas kernels  82.1 us (99%)
    pallas_call x1, Pallas kernels, local(): pl.pallas_call(kernel, out_shape=shapes, in_specs=[vmem] * 8, out_specs=(...  80.1 us
    pallas_call x1, Pallas kernels, local(): pl.pallas_call(hand_over, out_shape=shapes, in_specs=[whole] * 6, out_spe...  2.05 us

profile of v4, /device:TPU:64, one launch (start us, length us, event | category | flops | bytes accessed | tf_op | source)
XLA Modules:
  0.0 82.7 jit_solution(6280689401891862838)
XLA Ops:
  0.6 80.1 %shard_map.127 = (bf16[1,256,768]{2,1,0:T(8,128)(2,1)}, f32[1,256]{1,0:T(1,128)}, bf16[1,64,768]{2,1,0:T(8,128)(2,1)}, bf16[1,64,768]{2,1,0:T(8,128)(2,1)}, bf16...) custom-call(bf16[1,256,768]{2,1,0:T(8,128)(2,1)} %states.1, s32[1,256]{1,0:T(1,128)} %starts.1, f32[1,256]{1,0:T(1,128)} %conf.1, ...), custom_call_target="tpu_custom_call" | custom-call | flops 8000000000 | bytes 20000000 | tf_op jit(solution)/shard_map/pallas_call | solution.py:537
  80.7 2.0 %shard_map.128 = (bf16[1,256,768]{2,1,0:T(8,128)(2,1)}, f32[1,256]{1,0:T(1,128)}, bf16[1,64,768]{2,1,0:T(8,128)(2,1)}, bf16[1,64,768]{2,1,0:T(8,128)(2,1)}, bf16...) custom-call(bf16[1,256,768]{2,1,0:T(8,128)(2,1)} %get-tuple-element.12.refs_0_, f32[1,256]{1,0:T(1,128)} %get-tuple-element.13.refs_1_, ...), custom_call_target="tpu_custom_call" | custom-call | tf_op jit(solution)/shard_map/pallas_call | solution.py:617

commit v5 on v4

--- a/solution.py
+++ b/solution.py
@@ -33,8 +33,9 @@
 
 
 def kernel(
-    states, starts, conf, q_in, k_in, v_in, w_in, up,
-    byte_grad, conf_grad, dq_out, dk_out, dv_out, wg_out,
+    states_h, starts, conf, q_h, k_h, v_h, w_h, up_h,
+    byte_out, conf_grad, dq_out, dkv, wg_out,
+    states, q_in, k_in, v_in, w_in, up, byte_grad, in_sems, out_sems,
     stage, kv, wq, gext, spill_in, perm, pack, gp, gr, gq, dop, dr, og, dob,
     kt, vt, kkb, probs, inv, a_out, ab, pp, p1, ps4, pr, wgp, wgs, wg0, wh, wg1, rl, rs, wsum,
     lrow, prow, cpart, call, dqb, acc, sib, dkf, sel_s, grows,
@@ -42,7 +43,7 @@
     sp_send, sp_recv, g_send, g_recv, gx_send, gx_recv, dr_send, dr_recv,
     do_send, do_recv, a_send, a_recv, ay_send, ay_recv, px_send, px_recv, p_send, p_recv,
     w0_send, w0_recv, w1_send, w1_recv, rl_send, rl_recv, ws_send, ws_recv,
-    lr_send, lr_recv, c_send, c_recv, dq_send, dq_recv, dk_send, dk_recv, dv_send, dv_recv,
+    lr_send, lr_recv, c_send, c_recv, dq_send, dq_recv, dk_send, dk_recv,
     ex_send, ex_recv,
 ):
     s = lax.axis_index("seq")
@@ -145,7 +146,7 @@
 
     def a_flow(op, mm):
         for k in range(2):
-            op(a_out.at[mm, k], ab.at[lax.rem(mm, 4), :, lanes(att_h)], a_send.at[mm * 2 + k], a_recv,
+            op(a_out.at[mm, k], ab.at[lax.rem(mm, 4), :, lanes(att_h)], a_send, a_recv,
                (8 * (2 * r + k) + mm, x, att_w))
 
     def ay_flow(op):
@@ -182,12 +183,11 @@
 
     def dq_flow(op, mm):
         for k in range(2):
-            op(dqb.at[mm, k], dq_out.at[0, :, lanes(att_h)], dq_send.at[mm * 2 + k], dq_recv,
+            op(dqb.at[mm, k], dq_out.at[0, :, lanes(att_h)], dq_send, dq_recv,
                (8 * (2 * r + k) + mm, x, att_w))
 
     def dkv_flow(op, j):
-        op(dkf.at[0, j], dk_out.at[0, :, lanes(att_h)], dk_send.at[j], dk_recv, (16 * r + j, x, att_w))
-        op(dkf.at[1, j], dv_out.at[0, :, lanes(att_h)], dv_send.at[j], dv_recv, (16 * r + j, x, att_w))
+        op(dkf.at[j], dkv.at[:, :, lanes(att_h)], dk_send, dk_recv, (16 * r + j, x, att_w))
 
     def fw_flow(op):
         part = kv.at[pl.ds(16 * r, 16), pl.ds(0, 144)]
@@ -196,6 +196,14 @@
     spill_copy = remote(gext.at[pl.ds(64, 8)], spill_in, sp_send, sp_recv, (s - 1, x, r))
     row_copy = remote(lrow, prow, lr_send, lr_recv, (s + 1, x, r))
     ex_copy = remote(acc.at[1 - r], sib, ex_send, ex_recv, sib_id)
+
+    loads = [
+        pltpu.make_async_copy(there, here, in_sems.at[i])
+        for i, (there, here) in enumerate(
+            ((k_h, k_in), (v_h, v_in), (q_h, q_in), (w_h, w_in), (up_h, up), (states_h, states)))
+    ]
+    for load in loads:
+        load.start()
 
     barrier = pltpu.get_barrier_semaphore()
 
@@ -233,6 +241,8 @@
 
         lax.fori_loop(0, NS, one, 0)
 
+    for load in loads:
+        load.wait()
     start_row = starts[...].astype(F32)
     before = lax.broadcasted_iota(jnp.int32, (NB, NB), 0) <= lax.broadcasted_iota(jnp.int32, (NB, NB), 1)
     tri = jnp.where(before, 1.0, 0.0).astype(BF16)
@@ -300,6 +310,8 @@
     g_flow(send)
     g_lo = (group_grad - g_hi.astype(F32)).astype(BF16)
     byte_grad[0] = (upstream.astype(F32) + nn(picked_t, g_hi) + nn(picked_t, g_lo)).astype(BF16)
+    byte_copy = pltpu.make_async_copy(byte_grad, byte_out, out_sems.at[0])
+    byte_copy.start()
 
     landed(gr, g_recv)
     gathered = jnp.concatenate([gr[0], gr[1], gr[2], gr[3]], axis=1)
@@ -382,25 +394,6 @@
     w0_flow(start)
 
 
-    landed(wg0, w0_recv)
-    wh[...] = (wgp[:, mine48] + wg0[...].astype(F32)).astype(BF16)
-    w1_flow(start)
-
-    landed(p1.at[pl.ds(0, 3)], px_recv)
-    p1[x] = pp[x]
-    summed = (p1[0].astype(F32) + p1[1].astype(F32) + p1[2].astype(F32) + p1[3].astype(F32)).astype(BF16)
-    apart = nn(summed, pack[...]).astype(BF16)
-    for i in range(4):
-        ps4[i] = apart[:, 256 * i:256 * (i + 1)]
-    p_flow(send)
-
-    for j in range(3):
-        landed(rl.at[j], rl_recv.at[j])
-    far = rl[2].astype(F32)
-    rs[0] = (wh[z_place(2)].astype(F32) + rl[0].astype(F32) + jnp.where(even, far, 0.0)).astype(BF16)
-    rs[1] = (wh[z_place(6)].astype(F32) + rl[1].astype(F32) + jnp.where(even, 0.0, far)).astype(BF16)
-    w2_flow(start)
-
     @pl.when(is_att)
     def _():
         landed(dob, do_recv)
@@ -431,9 +424,31 @@
 
         lax.fori_loop(0, 4, backward, 0)
         ex_copy.start()
+
+    landed(wg0, w0_recv)
+    wh[...] = (wgp[:, mine48] + wg0[...].astype(F32)).astype(BF16)
+    w1_flow(start)
+
+    landed(p1.at[pl.ds(0, 3)], px_recv)
+    p1[x] = pp[x]
+    summed = (p1[0].astype(F32) + p1[1].astype(F32) + p1[2].astype(F32) + p1[3].astype(F32)).astype(BF16)
+    apart = nn(summed, pack[...]).astype(BF16)
+    for i in range(4):
+        ps4[i] = apart[:, 256 * i:256 * (i + 1)]
+    p_flow(send)
+
+    for j in range(3):
+        landed(rl.at[j], rl_recv.at[j])
+    far = rl[2].astype(F32)
+    rs[0] = (wh[z_place(2)].astype(F32) + rl[0].astype(F32) + jnp.where(even, far, 0.0)).astype(BF16)
+    rs[1] = (wh[z_place(6)].astype(F32) + rl[1].astype(F32) + jnp.where(even, 0.0, far)).astype(BF16)
+    w2_flow(start)
+
+    @pl.when(is_att)
+    def _():
         ex_copy.wait_recv()
-        dkf[0] = ((acc[r, 0] + sib[0]) * SCALE).T.astype(BF16).reshape(16, 64, HEAD_DIM)
-        dkf[1] = (acc[r, 1] + sib[1]).T.astype(BF16).reshape(16, 64, HEAD_DIM)
+        dkf[:, 0] = ((acc[r, 0] + sib[0]) * SCALE).T.astype(BF16).reshape(16, 64, HEAD_DIM)
+        dkf[:, 1] = (acc[r, 1] + sib[1]).T.astype(BF16).reshape(16, 64, HEAD_DIM)
 
         def out(step, _):
             dkv_flow(send, lax.rem(step + 3 * att, 16))
@@ -467,7 +482,8 @@
         total_w = total_w + wg1[j].astype(F32)
     wsum[...] = total_w
     ws_flow(start)
-    wg_out[mine48] = wsum[...]
+    wg_copy = pltpu.make_async_copy(wsum, wg_out.at[mine48], out_sems.at[1])
+    wg_copy.start()
 
     landed(call.at[pl.ds(0, 3)], c_recv)
     conf_grad[...] = (call[0] + call[1] + call[2] + call[3])[0:1]
@@ -493,28 +509,25 @@
         fw_flow(finish)
         ex_copy.wait_send()
 
-        def one(j, _):
-            a_flow(sent, j)
-            dq_flow(sent, j)
-            return 0
-
-        lax.fori_loop(0, 8, one, 0)
-
-        def two(j, _):
-            dkv_flow(sent, j)
-            return 0
-
-        lax.fori_loop(0, 16, two, 0)
+        own = jnp.logical_and(att_w == r, half == r)
+        for count_of, there in ((15, own), (16, jnp.logical_not(own))):
+            @pl.when(there)
+            def _(count_of=count_of):
+                landed(kv.at[pl.ds(0, count_of), pl.ds(0, 64)], a_send)
+                landed(kv.at[pl.ds(0, count_of), pl.ds(0, 64)], dq_send)
+                landed(kv.at[pl.ds(0, count_of), pl.ds(0, 128)], dk_send)
 
     landed(dq_out, dq_recv)
-    landed(dk_out, dk_recv)
-    landed(dv_out, dv_recv)
-
-
-def hand_over(*refs):
-    held, sems = refs[12:18], refs[18]
-    come = [pltpu.make_async_copy(refs[i], held[i], sems.at[i]) for i in range(6)]
-    leave = [pltpu.make_async_copy(held[i], refs[6 + i], sems.at[6 + i]) for i in range(6)]
+    landed(dkv, dk_recv)
+    byte_copy.wait()
+    wg_copy.wait()
+
+
+def hand_over(byte_in, conf_in, dq_in, dkv_in, wg_in, *refs):
+    outs, held, sems = refs[:6], refs[6:12], refs[12]
+    come = [byte_in, conf_in, dq_in, dkv_in.at[pl.ds(0, 1)], dkv_in.at[pl.ds(1, 1)], wg_in]
+    come = [pltpu.make_async_copy(come[i], held[i], sems.at[i]) for i in range(6)]
+    leave = [pltpu.make_async_copy(held[i], outs[i], sems.at[6 + i]) for i in range(6)]
     for copy in come:
         copy.start()
     for i in range(6):
@@ -526,6 +539,7 @@
 
 def local(byte_states, boundary, confidence, query_rows, key_rows, value_rows, out_weight, upstream):
     vmem = pl.BlockSpec(memory_space=pltpu.VMEM)
+    whole = pl.BlockSpec(memory_space=pl.ANY)
     dma = pltpu.SemaphoreType.DMA
     rows = jax.ShapeDtypeStruct((1, CAP, D), BF16)
     shapes = (
@@ -536,10 +550,18 @@
     )
     parts = pl.pallas_call(
         kernel,
-        out_shape=shapes,
-        in_specs=[vmem] * 8,
-        out_specs=(vmem,) * 6,
+        out_shape=(*shapes[:3], jax.ShapeDtypeStruct((2, CAP, D), BF16), shapes[5]),
+        in_specs=[whole, vmem, vmem] + [whole] * 5,
+        out_specs=(whole, vmem, whole, whole, whole),
         scratch_shapes=[
+            pltpu.VMEM((1, NB, D), BF16),
+            pltpu.VMEM((1, CAP, D), BF16),
+            pltpu.VMEM((1, CAP, D), BF16),
+            pltpu.VMEM((1, CAP, D), BF16),
+            pltpu.VMEM((96, D), BF16),
+            pltpu.VMEM((1, NB, D), BF16),
+            pltpu.VMEM((1, NB, D), BF16),
+            dma((6,)), dma((2,)),
             pltpu.VMEM((NH, 208, 128), BF16),
             pltpu.VMEM((NS, 208, 128), BF16),
             pltpu.VMEM((8, 96, D), BF16),
@@ -580,7 +602,7 @@
             pltpu.VMEM((8, 2, 64, 128), BF16),
             pltpu.VMEM((2, 2, 128, 1024), F32),
             pltpu.VMEM((2, 128, 1024), F32),
-            pltpu.VMEM((2, 16, 64, 128), BF16),
+            pltpu.VMEM((16, 2, 64, 128), BF16),
             pltpu.VMEM((80, NB), F32),
             pltpu.VMEM((64, D), F32),
             dma((6,)), dma,
@@ -593,7 +615,7 @@
             dma((3,)), dma,
             dma((3,)), dma,
             dma((6,)), dma,
-            dma((16,)), dma,
+            dma, dma,
             dma((3,)), dma,
             dma((3,)), dma,
             dma((4,)), dma,
@@ -603,9 +625,8 @@
             dma, dma,
             dma, dma,
             dma((3,)), dma,
-            dma((16,)), dma,
-            dma((16,)), dma,
-            dma((16,)), dma,
+            dma, dma,
+            dma, dma,
             dma, dma,
         ],
         compiler_params=pltpu.CompilerParams(
@@ -613,11 +634,10 @@
         ),
         cost_estimate=pl.CostEstimate(flops=8_000_000_000, bytes_accessed=20_000_000, transcendentals=3_000_000),
     )(byte_states, boundary, confidence, query_rows, key_rows, value_rows, out_weight, upstream)
-    whole = pl.BlockSpec(memory_space=pl.ANY)
     return pl.pallas_call(
         hand_over,
         out_shape=shapes,
-        in_specs=[whole] * 6,
+        in_specs=[whole] * 5,
         out_specs=(whole,) * 6,
         scratch_shapes=[pltpu.VMEM(shape.shape, shape.dtype) for shape in shapes] + [dma((12,))],
         compiler_params=pltpu.CompilerParams(vmem_limit_bytes=60 * 1024 * 1024),

time: 82.9 us -> 81.9 us (0.988)
  the two profiles are of different devices: /device:TPU:64 before, /device:TPU:66 now
where the time goes in v5:
time: 81.9 us; the launch traced here: 81.8 us
  Pallas kernels  81.1 us (99%)
    pallas_call x1, Pallas kernels, local(): pl.pallas_call(kernel, out_shape=(*shapes[:3], jax.ShapeDtypeStruct((2, C...  79.1 us
    pallas_call x1, Pallas kernels, local(): pl.pallas_call(hand_over, out_shape=shapes, in_specs=[whole] * 5, out_spe...  2.05 us

profile of v5, /device:TPU:66, one launch (start us, length us, event | category | flops | bytes accessed | tf_op | source)
XLA Modules:
  0.0 81.8 jit_solution(5301887492291994998)
XLA Ops:
  0.6 79.1 %shard_map.127 = (bf16[1,256,768]{2,1,0:T(8,128)(2,1)}, f32[1,256]{1,0:T(1,128)}, bf16[1,64,768]{2,1,0:T(8,128)(2,1)}, bf16[2,64,768]{2,1,0:T(8,128)(2,1)}, f32[96,768]{1,0:T(8,128)}) custom-call(bf16[1,256,768]{2,1,0:T(8,128)(2,1)} %states_h.1, s32[1,256]{1,0:T(1,128)} %starts.1, f32[1,256]{1,0:T(1,128)} %conf.1, bf16[1,64,768]{2,1,0:T(8,128)(2,1)} %q_h.1, ...), custom_call_target="tpu_custom_call" | custom-call | flops 8000000000 | bytes 20000000 | tf_op jit(solution)/shard_map/pallas_call | solution.py:551
  79.7 2.0 %shard_map.128 = (bf16[1,256,768]{2,1,0:T(8,128)(2,1)}, f32[1,256]{1,0:T(1,128)}, bf16[1,64,768]{2,1,0:T(8,128)(2,1)}, bf16[1,64,768]{2,1,0:T(8,128)(2,1)}, bf16...) custom-call(bf16[1,256,768]{2,1,0:T(8,128)(2,1)} %get-tuple-element.11.byte_in, f32[1,256]{1,0:T(1,128)} %get-tuple-element.12.conf_in, ...), custom_call_target="tpu_custom_call" | custom-call | tf_op jit(solution)/shard_map/pallas_call | solution.py:637

commit v6 on v5

--- a/solution.py
+++ b/solution.py
@@ -33,12 +33,11 @@
 
 
 def kernel(
-    states_h, starts, conf, q_h, k_h, v_h, w_h, up_h,
-    byte_out, conf_grad, dq_out, dkv, wg_out,
-    states, q_in, k_in, v_in, w_in, up, byte_grad, in_sems, out_sems,
+    states, starts, conf, q_in, k_in, v_in, w_in, up,
+    byte_grad, conf_grad, dq_out, dk_out, dv_out, wg_out,
     stage, kv, wq, gext, spill_in, perm, pack, gp, gr, gq, dop, dr, og, dob,
     kt, vt, kkb, probs, inv, a_out, ab, pp, p1, ps4, pr, wgp, wgs, wg0, wh, wg1, rl, rs, wsum,
-    lrow, prow, cpart, call, dqb, acc, sib, dkf, sel_s, grows,
+    lrow, prow, cpart, call, dqb, acc, sib, dkf, dkv, sel_s, grows,
     kv_send, kv_recv, fw_send, fw_recv, wa_send, wa_recv, wb_send, wb_recv, wd_send, wd_recv,
     sp_send, sp_recv, g_send, g_recv, gx_send, gx_recv, dr_send, dr_recv,
     do_send, do_recv, a_send, a_recv, ay_send, ay_recv, px_send, px_recv, p_send, p_recv,
@@ -197,14 +196,6 @@
     row_copy = remote(lrow, prow, lr_send, lr_recv, (s + 1, x, r))
     ex_copy = remote(acc.at[1 - r], sib, ex_send, ex_recv, sib_id)
 
-    loads = [
-        pltpu.make_async_copy(there, here, in_sems.at[i])
-        for i, (there, here) in enumerate(
-            ((k_h, k_in), (v_h, v_in), (q_h, q_in), (w_h, w_in), (up_h, up), (states_h, states)))
-    ]
-    for load in loads:
-        load.start()
-
     barrier = pltpu.get_barrier_semaphore()
 
     def greet(t):
@@ -241,8 +232,6 @@
 
         lax.fori_loop(0, NS, one, 0)
 
-    for load in loads:
-        load.wait()
     start_row = starts[...].astype(F32)
     before = lax.broadcasted_iota(jnp.int32, (NB, NB), 0) <= lax.broadcasted_iota(jnp.int32, (NB, NB), 1)
     tri = jnp.where(before, 1.0, 0.0).astype(BF16)
@@ -263,18 +252,7 @@
         stage[h, 64:128] = v_in[0, :, cols]
         stage[h, 128:144] = jnp.broadcast_to(count, (16, HEAD_DIM)).astype(BF16)
         stage[h, 144:208] = q_in[0, :, cols]
-    picked = sel[0:64] * start_row
-    picked_t = picked.T.astype(BF16)
-    grows[...] = nn(picked.astype(BF16), states[0])
     wq[z, mine48] = w_in[mine48]
-    last = lax.broadcasted_iota(jnp.int32, (64, D), 0).astype(F32) == count - 1.0
-    place = lax.broadcasted_iota(jnp.int32, (1, 1024), 1)
-    group, at = lax.div(place, 256), lax.rem(place, 256)
-    source = jnp.where(at < 96, 96 * group + at, jnp.where(at < 192, 96 * group + 288 + at, -1))
-    perm[...] = jnp.where(lax.broadcasted_iota(jnp.int32, (D, 1024), 0) == source, 1.0, 0.0).astype(BF16)
-    packed = jnp.where(at < 192, 192 * group + at, -1)
-    pack[...] = jnp.where(lax.broadcasted_iota(jnp.int32, (D, 1024), 0) == packed, 1.0, 0.0).astype(BF16)
-
     @pl.when(s == NS - 1)
     def _():
         spill_in[...] = jnp.zeros_like(spill_in)
@@ -298,6 +276,17 @@
     kv_flow(send)
     wa_flow(start)
 
+    place = lax.broadcasted_iota(jnp.int32, (1, 1024), 1)
+    group, at = lax.div(place, 256), lax.rem(place, 256)
+    source = jnp.where(at < 96, 96 * group + at, jnp.where(at < 192, 96 * group + 288 + at, -1))
+    perm[...] = jnp.where(lax.broadcasted_iota(jnp.int32, (D, 1024), 0) == source, 1.0, 0.0).astype(BF16)
+    packed = jnp.where(at < 192, 192 * group + at, -1)
+    pack[...] = jnp.where(lax.broadcasted_iota(jnp.int32, (D, 1024), 0) == packed, 1.0, 0.0).astype(BF16)
+    picked = sel[0:64] * start_row
+    picked_t = picked.T.astype(BF16)
+    grows[...] = nn(picked.astype(BF16), states[0])
+    last = lax.broadcasted_iota(jnp.int32, (64, D), 0).astype(F32) == count - 1.0
+
     @pl.when(s < NS - 1)
     def _():
         spill_copy.wait_recv()
@@ -308,18 +297,15 @@
     for i in range(4):
         gp[i] = spread[:, 256 * i:256 * (i + 1)]
     g_flow(send)
-    g_lo = (group_grad - g_hi.astype(F32)).astype(BF16)
-    byte_grad[0] = (upstream.astype(F32) + nn(picked_t, g_hi) + nn(picked_t, g_lo)).astype(BF16)
-    byte_copy = pltpu.make_async_copy(byte_grad, byte_out, out_sems.at[0])
-    byte_copy.start()
-
+    for j in (2, 3):
+        landed(w_in.at[pl.ds(0, 48)], wa_recv.at[j])
+    wb_flow(start)
     landed(gr, g_recv)
     gathered = jnp.concatenate([gr[0], gr[1], gr[2], gr[3]], axis=1)
     gq[x] = nt(gathered, pack[...]).astype(BF16)
     gx_flow(start)
-    for j in (2, 3):
-        landed(w_in.at[pl.ds(0, 48)], wa_recv.at[j])
-    wb_flow(start)
+    g_lo = (group_grad - g_hi.astype(F32)).astype(BF16)
+    byte_grad[0] = (upstream.astype(F32) + nn(picked_t, g_hi) + nn(picked_t, g_lo)).astype(BF16)
 
     @pl.when(is_att)
     def _():
@@ -482,8 +468,7 @@
         total_w = total_w + wg1[j].astype(F32)
     wsum[...] = total_w
     ws_flow(start)
-    wg_copy = pltpu.make_async_copy(wsum, wg_out.at[mine48], out_sems.at[1])
-    wg_copy.start()
+    wg_out[mine48] = wsum[...]
 
     landed(call.at[pl.ds(0, 3)], c_recv)
     conf_grad[...] = (call[0] + call[1] + call[2] + call[3])[0:1]
@@ -519,15 +504,14 @@
 
     landed(dq_out, dq_recv)
     landed(dkv, dk_recv)
-    byte_copy.wait()
-    wg_copy.wait()
-
-
-def hand_over(byte_in, conf_in, dq_in, dkv_in, wg_in, *refs):
-    outs, held, sems = refs[:6], refs[6:12], refs[12]
-    come = [byte_in, conf_in, dq_in, dkv_in.at[pl.ds(0, 1)], dkv_in.at[pl.ds(1, 1)], wg_in]
-    come = [pltpu.make_async_copy(come[i], held[i], sems.at[i]) for i in range(6)]
-    leave = [pltpu.make_async_copy(held[i], outs[i], sems.at[6 + i]) for i in range(6)]
+    dk_out[0] = dkv[0]
+    dv_out[0] = dkv[1]
+
+
+def hand_over(*refs):
+    held, sems = refs[12:18], refs[18]
+    come = [pltpu.make_async_copy(refs[i], held[i], sems.at[i]) for i in range(6)]
+    leave = [pltpu.make_async_copy(held[i], refs[6 + i], sems.at[6 + i]) for i in range(6)]
     for copy in come:
         copy.start()
     for i in range(6):
@@ -539,7 +523,6 @@
 
 def local(byte_states, boundary, confidence, query_rows, key_rows, value_rows, out_weight, upstream):
     vmem = pl.BlockSpec(memory_space=pltpu.VMEM)
-    whole = pl.BlockSpec(memory_space=pl.ANY)
     dma = pltpu.SemaphoreType.DMA
     rows = jax.ShapeDtypeStruct((1, CAP, D), BF16)
     shapes = (
@@ -550,18 +533,10 @@
     )
     parts = pl.pallas_call(
         kernel,
-        out_shape=(*shapes[:3], jax.ShapeDtypeStruct((2, CAP, D), BF16), shapes[5]),
-        in_specs=[whole, vmem, vmem] + [whole] * 5,
-        out_specs=(whole, vmem, whole, whole, whole),
+        out_shape=shapes,
+        in_specs=[vmem] * 8,
+        out_specs=(vmem,) * 6,
         scratch_shapes=[
-            pltpu.VMEM((1, NB, D), BF16),
-            pltpu.VMEM((1, CAP, D), BF16),
-            pltpu.VMEM((1, CAP, D), BF16),
-            pltpu.VMEM((1, CAP, D), BF16),
-            pltpu.VMEM((96, D), BF16),
-            pltpu.VMEM((1, NB, D), BF16),
-            pltpu.VMEM((1, NB, D), BF16),
-            dma((6,)), dma((2,)),
             pltpu.VMEM((NH, 208, 128), BF16),
             pltpu.VMEM((NS, 208, 128), BF16),
             pltpu.VMEM((8, 96, D), BF16),
@@ -603,6 +578,7 @@
             pltpu.VMEM((2, 2, 128, 1024), F32),
             pltpu.VMEM((2, 128, 1024), F32),
             pltpu.VMEM((16, 2, 64, 128), BF16),
+            pltpu.VMEM((2, 64, D), BF16),
             pltpu.VMEM((80, NB), F32),
             pltpu.VMEM((64, D), F32),
             dma((6,)), dma,
@@ -634,10 +610,11 @@
         ),
         cost_estimate=pl.CostEstimate(flops=8_000_000_000, bytes_accessed=20_000_000, transcendentals=3_000_000),
     )(byte_states, boundary, confidence, query_rows, key_rows, value_rows, out_weight, upstream)
+    whole = pl.BlockSpec(memory_space=pl.ANY)
     return pl.pallas_call(
         hand_over,
         out_shape=shapes,
-        in_specs=[whole] * 5,
+        in_specs=[whole] * 6,
         out_specs=(whole,) * 6,
         scratch_shapes=[pltpu.VMEM(shape.shape, shape.dtype) for shape in shapes] + [dma((12,))],
         compiler_params=pltpu.CompilerParams(vmem_limit_bytes=60 * 1024 * 1024),

time: 81.9 us -> 79.9 us (0.976)
  the two profiles are of different devices: /device:TPU:66 before, /device:TPU:68 now
where the time goes in v6:
time: 79.9 us; the launch traced here: 79.7 us
  Pallas kernels  79.1 us (99%)
    pallas_call x1, Pallas kernels, local(): pl.pallas_call(kernel, out_shape=shapes, in_specs=[vmem] * 8, out_specs=(...  77.1 us
    pallas_call x1, Pallas kernels, local(): pl.pallas_call(hand_over, out_shape=shapes, in_specs=[whole] * 6, out_spe...  2.05 us

profile of v6, /device:TPU:68, one launch (start us, length us, event | category | flops | bytes accessed | tf_op | source)
XLA Modules:
  0.0 79.7 jit_solution(3137908166594862839)
XLA Ops:
  0.6 77.1 %shard_map.127 = (bf16[1,256,768]{2,1,0:T(8,128)(2,1)}, f32[1,256]{1,0:T(1,128)}, bf16[1,64,768]{2,1,0:T(8,128)(2,1)}, bf16[1,64,768]{2,1,0:T(8,128)(2,1)}, bf16...) custom-call(bf16[1,256,768]{2,1,0:T(8,128)(2,1)} %states.1, s32[1,256]{1,0:T(1,128)} %starts.1, f32[1,256]{1,0:T(1,128)} %conf.1, ...), custom_call_target="tpu_custom_call" | custom-call | flops 8000000000 | bytes 20000000 | tf_op jit(solution)/shard_map/pallas_call | solution.py:534
  77.7 2.0 %shard_map.128 = (bf16[1,256,768]{2,1,0:T(8,128)(2,1)}, f32[1,256]{1,0:T(1,128)}, bf16[1,64,768]{2,1,0:T(8,128)(2,1)}, bf16[1,64,768]{2,1,0:T(8,128)(2,1)}, bf16...) custom-call(bf16[1,256,768]{2,1,0:T(8,128)(2,1)} %get-tuple-element.12.refs_0_, f32[1,256]{1,0:T(1,128)} %get-tuple-element.13.refs_1_, ...), custom_call_target="tpu_custom_call" | custom-call | tf_op jit(solution)/shard_map/pallas_call | solution.py:614

commit v7 on v6

--- a/solution.py
+++ b/solution.py
@@ -430,17 +430,6 @@
     rs[1] = (wh[z_place(6)].astype(F32) + rl[1].astype(F32) + jnp.where(even, 0.0, far)).astype(BF16)
     w2_flow(start)
 
-    @pl.when(is_att)
-    def _():
-        ex_copy.wait_recv()
-        dkf[:, 0] = ((acc[r, 0] + sib[0]) * SCALE).T.astype(BF16).reshape(16, 64, HEAD_DIM)
-        dkf[:, 1] = (acc[r, 1] + sib[1]).T.astype(BF16).reshape(16, 64, HEAD_DIM)
-
-        def out(step, _):
-            dkv_flow(send, lax.rem(step + 3 * att, 16))
-            return 0
-
-        lax.fori_loop(0, 16, out, 0)
     landed(pr, p_recv)
     gathered = jnp.concatenate([pr[0], pr[1], pr[2], pr[3]], axis=1)
     group_out = (grows[...] + nt(gathered, perm[...])).astype(BF16)
@@ -452,6 +441,17 @@
     def _():
         row_copy.start()
 
+    @pl.when(is_att)
+    def _():
+        ex_copy.wait_recv()
+        dkf[:, 0] = ((acc[r, 0] + sib[0]) * SCALE).T.astype(BF16).reshape(16, 64, HEAD_DIM)
+        dkf[:, 1] = (acc[r, 1] + sib[1]).T.astype(BF16).reshape(16, 64, HEAD_DIM)
+
+        def out(step, _):
+            dkv_flow(send, lax.rem(step + 3 * att, 16))
+            return 0
+
+        lax.fori_loop(0, 16, out, 0)
     @pl.when(s > 0)
     def _():
         row_copy.wait_recv()

time: 79.9 us -> 79.9 us (level)
  no operation moved by 1% of the time
where the time goes in v7:
time: 79.9 us; the launch traced here: 79.7 us
  Pallas kernels  79.1 us (99%)
    pallas_call x1, Pallas kernels, local(): pl.pallas_call(kernel, out_shape=shapes, in_specs=[vmem] * 8, out_specs=(...  77.1 us
    pallas_call x1, Pallas kernels, local(): pl.pallas_call(hand_over, out_shape=shapes, in_specs=[whole] * 6, out_spe...  2.05 us

profile of v7, /device:TPU:68, one launch (start us, length us, event | category | flops | bytes accessed | tf_op | source)
XLA Modules:
  0.0 79.7 jit_solution(9089704004148055970)
XLA Ops:
  0.6 77.1 %shard_map.127 = (bf16[1,256,768]{2,1,0:T(8,128)(2,1)}, f32[1,256]{1,0:T(1,128)}, bf16[1,64,768]{2,1,0:T(8,128)(2,1)}, bf16[1,64,768]{2,1,0:T(8,128)(2,1)}, bf16...) custom-call(bf16[1,256,768]{2,1,0:T(8,128)(2,1)} %states.1, s32[1,256]{1,0:T(1,128)} %starts.1, f32[1,256]{1,0:T(1,128)} %conf.1, ...), custom_call_target="tpu_custom_call" | custom-call | flops 8000000000 | bytes 20000000 | tf_op jit(solution)/shard_map/pallas_call | solution.py:534
  77.7 2.0 %shard_map.128 = (bf16[1,256,768]{2,1,0:T(8,128)(2,1)}, f32[1,256]{1,0:T(1,128)}, bf16[1,64,768]{2,1,0:T(8,128)(2,1)}, bf16[1,64,768]{2,1,0:T(8,128)(2,1)}, bf16...) custom-call(bf16[1,256,768]{2,1,0:T(8,128)(2,1)} %get-tuple-element.12.refs_0_, f32[1,256]{1,0:T(1,128)} %get-tuple-element.13.refs_1_, ...), custom_call_target="tpu_custom_call" | custom-call | tf_op jit(solution)/shard_map/pallas_call | solution.py:614
